TPU v7x, 128 devices: a whole 4x4x4 slice. The times are simulated.
128 devices in a mesh: fsdp: 16 (over y, z), tp: 8 (over x, core).
Axes of the slice: x: 4, y: 4, z: 4, core: 2. Of those that a mesh axis runs over, the one named last changes fastest.
Arguments:
- gradient: bfloat16 [8192, 14336], P('fsdp', 'tp'), may hold values from -6 to 6
- momentum: float32 [8192, 14336], P('fsdp', 'tp')
- basis: float32 [14336, 1024], P(('tp', 'fsdp')), may hold values from -0.046875 to 0.046875
Outputs:
- new_momentum: float32 [8192, 14336], P('fsdp', 'tp')
- new_basis: float32 [14336, 1024], P(('tp', 'fsdp'))
- update: bfloat16 [8192, 14336], P('fsdp', 'tp')
All inputs are finite; a program needn't handle non-finite values.
Results may differ from a plain program's by a relative error of at most 0.0023.
Values sent between devices are 32-bit elements; how exact they have to be, the bound alone decides.
A program may use at most 128 MiB of HBM per device.

v0:
```python
import jax
import jax.numpy as jnp
from jax import lax
from jax.sharding import PartitionSpec as P

M = 8192
N = 14336
RANK = 1024


def mmul(a, b):
    return jnp.dot(a, b, precision=lax.Precision.HIGHEST, preferred_element_type=jnp.float32)


def local(gradient, momentum, basis):
    mixed = momentum + gradient.astype(jnp.float32)
    row_count = mixed.shape[0]
    columns = mixed
    partial_left = mmul(columns, lax.all_gather(basis, "fsdp", axis=0, tiled=True))
    left = lax.psum(partial_left, "tp")
    gram = lax.psum(mmul(left.T, left), "fsdp")
    lower = jnp.linalg.cholesky(gram)
    ortho = lax.linalg.triangular_solve(lower, left, left_side=False, lower=True, transpose_a=True)
    factor = jnp.sqrt(jnp.float32(M) * jnp.float32(N) / jnp.float32(RANK))
    columns = mixed
    right_mine = lax.psum_scatter(mmul(columns.T, ortho), "fsdp", scatter_dimension=0, tiled=True)
    squares = lax.psum(jnp.sum(right_mine * right_mine, axis=0), ("fsdp", "tp"))
    colnorm = jnp.sqrt(squares + 1e-08)
    new_basis = right_mine / colnorm
    stacked = jnp.concatenate([0.05 * ortho, factor * ortho / colnorm], axis=0)
    products = mmul(stacked, lax.all_gather(right_mine, "fsdp", axis=0, tiled=True).T)
    new_momentum = mixed - products[:row_count]
    update = products[row_count:].astype(jnp.bfloat16)
    return (new_momentum, new_basis, update)


def solution(mesh):
    placed = (P("fsdp", "tp"), P("fsdp", "tp"), P(("tp", "fsdp"), None))
    return jax.shard_map(
        local,
        mesh=mesh,
        in_specs=placed,
        out_specs=(P("fsdp", "tp"), P(("tp", "fsdp"), None), P("fsdp", "tp")),
        check_vma=False,
    )
```

profile of v0, /device:TPU:1, one launch (start us, length us, event | category | flops | bytes accessed | tf_op | source)
XLA Modules:
  0.0 880.1 jit_solution(6080029660072212431)
XLA Ops:
  7.9 71.8 %all-gather.3.cloned.1.call-done = f32[1792,1024]{1,0:T(8,128)} async-done(((f32[112,1024]{1,0:T(8,128)}), f32[1792,1024]{1,0:T(8,128)}) %all-gather.3.cloned.1.call-update) | async-done | bytes 7340048 | tf_op jit(solution)/shard_map/all_gather | solution.py:19
  79.7 16.9 %fusion.6 = f32[512,1024]{1,0:T(8,128)} fusion(f32[1792,1024]{1,0:T(8,128)} %all-gather.3.cloned.1.call-done, f32[512,1792]{1,0:T(8,128)} %param.4, bf16[512,1792]{1,0:T(8,128)(2,1)} %param.3), kind=kOutput, calls=%fused_computation.15 | convolution fusion | flops 11276124160 | bytes 14942208 | tf_op jit(solution)/shard_map/dot_general | solution.py:12
  96.7 63.4 %all-reduce.4.cloned.1.call-done = f32[512,1024]{1,0:T(8,128)} async-done(((f32[512,1024]{1,0:T(8,128)}), f32[512,1024]{1,0:T(8,128)}) %all-reduce.4.cloned.1.call-update) | async-done | bytes 2097168 | tf_op jit(solution)/shard_map/psum | solution.py:20
  160.1 10.3 %fusion.69 = f32[1024,1024]{0,1:T(8,128)} fusion(f32[512,1024]{1,0:T(8,128)} %all-reduce.4.cloned.1.call-done), kind=kOutput, calls=%fused_computation.170 | convolution fusion | flops 6442450944 | bytes 6291456 | tf_op jit(solution)/shard_map/dot_general | solution.py:12
  170.5 104.9 %all-reduce.6.cloned.1.call-done = f32[1024,1024]{0,1:T(8,128)} async-done(((f32[1024,1024]{0,1:T(8,128)}), f32[1024,1024]{0,1:T(8,128)}) %all-reduce.6.cloned.1.call-update) | async-done | bytes 4194320 | tf_op jit(solution)/shard_map/psum | solution.py:21
  287.3 11.7 %cholesky.223 = f32[128,128]{1,0:T(8,128)S(1)} custom-call(f32[128,128]{1,0:T(8,128)S(1)} %cholesky.580), custom_call_target="Cholesky" | custom-call | tf_op jit(solution)/shard_map/jit(cholesky)/cholesky | solution.py:22
  299.1 9.8 %custom-call.62 = f32[1,128,128]{1,2,0:T(8,128)S(1)} custom-call(f32[1,128,128]{2,1,0:T(8,128)S(1)} %get-tuple-element.69), custom_call_target="InvertDiagBlocksLowerTriangular" | custom-call | tf_op jit(solution)/shard_map/jit(cholesky)/cholesky | solution.py:22
  315.4 11.9 %cholesky.244 = f32[128,128]{1,0:T(8,128)S(1)} custom-call(f32[128,128]{1,0:T(8,128)S(1)} %cholesky.584), custom_call_target="Cholesky" | custom-call | tf_op jit(solution)/shard_map/jit(cholesky)/cholesky | solution.py:22
  327.9 9.8 %custom-call.63 = f32[1,128,128]{1,2,0:T(8,128)S(1)} custom-call(f32[1,128,128]{2,1,0:T(8,128)S(1)} %get-tuple-element.66), custom_call_target="InvertDiagBlocksLowerTriangular" | custom-call | tf_op jit(solution)/shard_map/jit(cholesky)/cholesky | solution.py:22
  341.1 11.7 %cholesky.468 = f32[128,128]{1,0:T(8,128)S(1)} custom-call(f32[128,128]{1,0:T(8,128)S(1)} %cholesky.589), custom_call_target="Cholesky" | custom-call | tf_op jit(solution)/shard_map/jit(cholesky)/cholesky | solution.py:22
  354.1 9.8 %custom-call.64 = f32[1,128,128]{1,2,0:T(8,128)S(1)} custom-call(f32[1,128,128]{2,1,0:T(8,128)S(1)} %get-tuple-element.63), custom_call_target="InvertDiagBlocksLowerTriangular" | custom-call | tf_op jit(solution)/shard_map/jit(cholesky)/cholesky | solution.py:22
  367.4 12.1 %cholesky.487 = f32[128,128]{1,0:T(8,128)S(1)} custom-call(f32[128,128]{1,0:T(8,128)S(1)} %cholesky.594), custom_call_target="Cholesky" | custom-call | tf_op jit(solution)/shard_map/jit(cholesky)/cholesky | solution.py:22
  380.8 9.8 %custom-call.65 = f32[1,128,128]{1,2,0:T(8,128)S(1)} custom-call(f32[1,128,128]{2,1,0:T(8,128)S(1)} %get-tuple-element.60), custom_call_target="InvertDiagBlocksLowerTriangular" | custom-call | tf_op jit(solution)/shard_map/jit(cholesky)/cholesky | solution.py:22
  394.1 11.7 %cholesky.506 = f32[128,128]{1,0:T(8,128)S(1)} custom-call(f32[128,128]{1,0:T(8,128)S(1)} %cholesky.599), custom_call_target="Cholesky" | custom-call | tf_op jit(solution)/shard_map/jit(cholesky)/cholesky | solution.py:22
  407.1 9.9 %custom-call.66 = f32[1,128,128]{1,2,0:T(8,128)S(1)} custom-call(f32[1,128,128]{2,1,0:T(8,128)S(1)} %get-tuple-element.57), custom_call_target="InvertDiagBlocksLowerTriangular" | custom-call | tf_op jit(solution)/shard_map/jit(cholesky)/cholesky | solution.py:22
  420.4 11.7 %cholesky.526 = f32[128,128]{1,0:T(8,128)S(1)} custom-call(f32[128,128]{1,0:T(8,128)S(1)} %cholesky.604), custom_call_target="Cholesky" | custom-call | tf_op jit(solution)/shard_map/jit(cholesky)/cholesky | solution.py:22
  446.2 12.1 %cholesky.546 = f32[128,128]{1,0:T(8,128)S(1)} custom-call(f32[128,128]{1,0:T(8,128)S(1)} %cholesky.609), custom_call_target="Cholesky" | custom-call | tf_op jit(solution)/shard_map/jit(cholesky)/cholesky | solution.py:22
  472.0 11.7 %cholesky.564 = f32[128,128]{1,0:T(8,128)S(1)} custom-call(f32[128,128]{1,0:T(8,128)S(1)} %convolution_subtract_fusion.13), custom_call_target="Cholesky" | custom-call | tf_op jit(solution)/shard_map/jit(cholesky)/cholesky | solution.py:22
  495.8 23.2 %while.1 = (s32[]{:T(128)}, f32[1024,1024]{1,0:T(8,128)}, s32[8,2]{0,1:T(2,128)S(1)}, f32[8,128,128]{2,1,0:T(8,128)S(1)}, s32[]{:T(128)}) while((s32[]{:T(128)}, f32[1024,1024]{1,0:T(8,128)}, s32[8,2]{0,1:T(2,128)S(1)}, f32[8,128,128]{2,1,0:T(8,128)S(1)}, s32[]{:T(128)}) %tuple.62), condition=%wide.while_cond, body=%wide.while_body.sunk | while | flops 2 | bytes 131189 | solution.py:23
  519.0 78.8 %custom-call.69 = f32[8,128,128]{1,2,0:T(8,128)S(1)} custom-call(f32[8,128,128]{2,1,0:T(8,128)S(1)} %get-tuple-element.10), custom_call_target="InvertDiagBlocksLowerTriangular" | custom-call | tf_op jit(solution)/shard_map/triangular_solve | solution.py:23
  622.4 25.3 %fusion.5 = f32[1792,1024]{1,0:T(8,128)} fusion(f32[512,1024]{0,1:T(8,128)S(1)} %convolution_dynamic-update-slice_fusion.2, f32[512,1792]{1,0:T(8,128)S(1)} %copy-done, bf16[512,1792]{1,0:T(8,128)(2,1)S(1)} %copy-done.3), kind=kOutput, calls=%fused_computation.14 | convolution fusion | flops 11276124160 | bytes 14942208 | tf_op jit(solution)/shard_map/dot_general | solution.py:12
  647.8 82.0 %reduce-scatter.2.cloned.1.call-done = f32[112,1024]{1,0:T(8,128)} async-done(((f32[1792,1024]{1,0:T(8,128)}), f32[112,1024]{1,0:T(8,128)}) %reduce-scatter.2.cloned.1.call-update) | async-done | bytes 458768 | tf_op jit(solution)/shard_map/reduce_scatter | solution.py:26
  730.9 66.6 %psum.23 = f32[1024]{0:T(1024)S(1)} all-reduce(f32[1024]{0:T(1024)S(1)} %multiply_reduce_fusion), channel_id=1, replica_groups=mesh['fsdp'=16,'tp'=8] {'fsdp','tp'}, use_global_device_ids=true, to_apply=%region_20.21 | all-reduce | flops 1024 | bytes 8192 | tf_op jit(solution)/shard_map/psum | solution.py:27
  801.8 66.2 %fusion = f32[1024,1792]{1,0:T(8,128)S(1)} fusion(f32[1792,1024]{1,0:T(8,128)} %all-gather.5.cloned.1.call-done, f32[512,1024]{0,1:T(8,128)} %get-tuple-element.22, f32[512,1024]{0,1:T(8,128)} %get-tuple-element.21), kind=kOutput, calls=%fused_computation.3 | convolution fusion | flops 22549626880 | bytes 18874368 | tf_op jit(solution)/shard_map/dot_general | solution.py:12
  (117 shorter events, 130.5 us)
Async XLA Ops:
  7.2 72.5 %all-gather.3.cloned.1.call-start = ((), (), s32[]{:S(2)}) async-start(), calls=%async_computation.1 | async-start | bytes 7798784 | tf_op jit(solution)/shard_map/all_gather | solution.py:19
  7.9 152.2 %all-reduce.4.cloned.1.call-start = ((), (), s32[]{:S(2)}) async-start(), calls=%async_computation.2 | async-start | bytes 4194304 | tf_op jit(solution)/shard_map/psum | solution.py:20
  96.7 178.8 %all-reduce.6.cloned.1.call-start = ((), (), s32[]{:S(2)}) async-start(), calls=%async_computation.3 | async-start | bytes 8388608 | tf_op jit(solution)/shard_map/psum | solution.py:21
  170.5 559.4 %reduce-scatter.2.cloned.1.call-start = ((), (), s32[]{:S(2)}) async-start(), calls=%async_computation.4 | async-start | bytes 7798784 | tf_op jit(solution)/shard_map/reduce_scatter | solution.py:26
  285.4 1.9 copy-start.5
  490.9 106.9 %copy-start.2 = (f32[512,1024]{1,0:T(8,128)S(1)}, f32[512,1024]{1,0:T(8,128)}, u32[]{:S(2)}) copy-start(f32[512,1024]{1,0:T(8,128)} %all-reduce.4.cloned.1.call-done) | copy-start | bytes 6291460
  611.9 10.6 %copy-start = (f32[512,1792]{1,0:T(8,128)S(1)}, f32[512,1792]{1,0:T(8,128)}, u32[]{:S(2)}) copy-start(f32[512,1792]{1,0:T(8,128)} %param.4) | copy-start | bytes 11010052
  611.9 10.6 %copy-start.3 = (bf16[512,1792]{1,0:T(8,128)(2,1)S(1)}, bf16[512,1792]{1,0:T(8,128)(2,1)}, u32[]{:S(2)}) copy-start(bf16[512,1792]{1,0:T(8,128)(2,1)} %param.3) | copy-start | bytes 5505028
  621.1 1.3 copy-start.6
  647.7 151.7 %copy-start.7 = (f32[512,1024]{0,1:T(8,128)S(1)}, f32[512,1024]{0,1:T(8,128)}, u32[]{:S(2)}) copy-start(f32[512,1024]{0,1:T(8,128)} %copy-done.6) | copy-start | bytes 6291460
  647.7 154.1 %all-gather.5.cloned.1.call-start = ((), (), s32[]{:S(2)}) async-start(), calls=%async_computation.5 | async-start | bytes 7798784 | tf_op jit(solution)/shard_map/all_gather | solution.py:31
  801.8 67.6 %copy-start.4 = (bf16[512,1792]{1,0:T(8,128)(2,1)S(1)}, bf16[512,1792]{1,0:T(8,128)(2,1)}, u32[]{:S(2)}) copy-start(bf16[512,1792]{1,0:T(8,128)(2,1)} %param.3) | copy-start | bytes 5505028
  868.0 2.7 copy-start.1
Sparse Core Ops, SparseCore 0:
  10.2 69.4 all-gather.2
  96.8 63.2 all-reduce.3
  170.6 104.8 all-reduce.5
  647.9 81.9 reduce-scatter.1
  732.1 67.8 all-gather.4
where the time goes:
time: 888 us; the launch traced here: 880 us
  waiting for transfers between devices  323 us (36%)
  other arithmetic  269 us (30%)
  matrix products  165 us (19%)
  blocking collectives  66.6 us (7%)
  local copies, waits for them, and re-layouts  37 us (4%)
  between operations  19.5 us (2%)
    another operation x30, other arithmetic, local(): lower = jnp.linalg.cholesky(gram)  173 us
    dot_general x4, matrix products, mmul(): jnp.dot(a, b, precision=lax.Precision.HIGHEST, preferred_element_type=jnp...  119 us
    psum x1, waiting for transfers between devices, local(): gram = lax.psum(mmul(left.T, left), 'fsdp')  105 us
    another operation x3, other arithmetic, local(): lax.linalg.triangular_solve(lower, left, left_side=False, lower=True, tra...  83.7 us
    reduce_scatter x1, waiting for transfers between devices, local(): lax.psum_scatter(mmul(columns.T, ortho), 'fsdp', scatter_dimension=0, til...  82 us
    all_gather x1, waiting for transfers between devices, local(): lax.all_gather(basis, 'fsdp', axis=0, tiled=True)  71.8 us
    psum x1, blocking collectives, local(): squares = lax.psum(jnp.sum(right_mine * right_mine, axis=0), ('fsdp', 'tp'))  66.6 us
    psum x1, waiting for transfers between devices, local(): left = lax.psum(partial_left, 'tp')  63.4 us
  transfers between devices with their start and end apart: 5, of which 4 were waited for; matrix products, arithmetic and copies ran while one was open for 1% of the time, Pallas kernels for 0%

commit v1 on v0

v1 whole, which is shorter than its diff:
```python
import functools

import jax
import jax.numpy as jnp
from jax import lax
from jax.experimental import pallas as pl
from jax.experimental.pallas import tpu as pltpu
from jax.sharding import PartitionSpec as P

M = 8192
N = 14336
RANK = 1024
BLOCK = 128
STRIP = 8
HIGHEST = lax.Precision.HIGHEST
HIGH = lax.Precision.HIGH


def dot(a, b, ca, cb, precision):
    dims = (((ca,), (cb,)), ((), ()))
    return lax.dot_general(a, b, dims, precision=precision, preferred_element_type=jnp.float32)


def recip(d):
    r = pl.reciprocal(d, approx=True)
    r = r * (2.0 - d * r)
    return r * (2.0 - d * r)


def factor(block):
    shape = (STRIP, BLOCK)
    lane = lax.broadcasted_iota(jnp.int32, shape, 1)
    sub = lax.broadcasted_iota(jnp.int32, shape, 0)
    count = BLOCK // STRIP
    strips = [block[STRIP * t : STRIP * (t + 1), :] for t in range(count)]
    out = []
    for s in range(count):
        first = STRIP * s
        w = strips[s]
        columns = [jnp.broadcast_to(w[:, first + j : first + j + 1], shape) for j in range(STRIP)]
        a = [[jnp.broadcast_to(columns[j][i : i + 1, :], shape) for j in range(i + 1)] for i in range(STRIP)]
        pivots = jnp.ones(shape, jnp.float32)
        for k in range(STRIP):
            here = lane == first + k
            inverse = recip(a[k][k])
            pivots = jnp.where(sub == k, a[k][k], pivots)
            ratio = {i: a[i][k] * inverse for i in range(k + 1, STRIP)}
            for i in range(k + 1, STRIP):
                for j in range(k + 1, i + 1):
                    a[i][j] = a[i][j] - ratio[i] * a[j][k]
            times = jnp.zeros(shape, jnp.float32)
            for i in range(k + 1, STRIP):
                times = jnp.where(sub == i, ratio[i], times)
            w = jnp.where(here & (sub >= k), jnp.where(sub == k, 1.0, 0.0), w)
            w = w - times * jnp.broadcast_to(w[k : k + 1, :], shape)
        r = w * lax.rsqrt(pivots)
        r = jnp.where((lane > first + sub) & (lane < first + STRIP), 0.0, r)
        out.append(jnp.where(lane <= sub + first, r, 0.0))
        inside = (lane >= first) & (lane < first + STRIP)
        turned = jnp.transpose(r)
        rows = [jnp.broadcast_to(r[i : i + 1, :], shape) for i in range(STRIP)]
        for t in range(s + 1, count):
            total = jnp.where(inside, 0.0, strips[t])
            for i in range(STRIP):
                total = total - jnp.broadcast_to(turned[STRIP * t : STRIP * (t + 1), i : i + 1], shape) * rows[i]
            strips[t] = total
    return jnp.concatenate(out, axis=0)


def inverse_kernel(gram_ref, out_ref, held):
    n = held.shape[0]
    held[...] = gram_ref[...]
    shape = (BLOCK, BLOCK)
    eye = (lax.broadcasted_iota(jnp.int32, shape, 0) == lax.broadcasted_iota(jnp.int32, shape, 1)).astype(jnp.float32)
    lanes = lax.broadcasted_iota(jnp.int32, (BLOCK, n), 1)

    def step(k, carry):
        mine = pl.ds(pl.multiple_of(k * BLOCK, BLOCK), BLOCK)
        inverse = factor(held[mine, mine])
        held[mine, mine] = eye
        held[mine, :] = dot(inverse, held[mine, :], 1, 0, HIGHEST)
        out_ref[mine, :] = jnp.where(lanes < (k + 1) * BLOCK, held[mine, :], 0.0)

        def below(t, inner):
            rows = pl.ds(pl.multiple_of(t * BLOCK, BLOCK), BLOCK)
            held[rows, mine] = jnp.zeros(shape, jnp.float32)
            held[rows, :] = held[rows, :] - dot(held[mine, rows], held[mine, :], 0, 0, HIGHEST)
            return inner

        lax.fori_loop(k + 1, n // BLOCK, below, 0)
        return carry

    lax.fori_loop(0, n // BLOCK, step, 0)


def cholesky_inverse(gram):
    return pl.pallas_call(
        inverse_kernel,
        out_shape=jax.ShapeDtypeStruct(gram.shape, jnp.float32),
        in_specs=[pl.BlockSpec(memory_space=pltpu.VMEM)],
        out_specs=pl.BlockSpec(memory_space=pltpu.VMEM),
        scratch_shapes=[pltpu.VMEM(gram.shape, jnp.float32)],
        compiler_params=pltpu.CompilerParams(vmem_limit_bytes=32 << 20),
        cost_estimate=pl.CostEstimate(flops=60_000_000_000, bytes_accessed=8 << 20, transcendentals=0),
        name="cholesky_inverse",
    )(gram)


def local(gradient, momentum, basis):
    mixed = momentum + gradient.astype(jnp.float32)
    left = lax.psum(dot(mixed, lax.all_gather(basis, "fsdp", axis=0, tiled=True), 1, 0, HIGH), "tp")
    part = lax.axis_index("tp") * BLOCK
    gram_part = dot(left, lax.dynamic_slice_in_dim(left, part, BLOCK, 1), 0, 0, HIGHEST)
    gram = lax.all_gather(lax.psum(gram_part.T, "fsdp"), "tp", axis=0, tiled=True)
    cross_mine = lax.psum_scatter(dot(mixed, left, 0, 0, HIGH), "fsdp", scatter_dimension=0, tiled=True)
    cross = lax.all_gather(cross_mine, "fsdp", axis=0, tiled=True)
    inverse = cholesky_inverse(gram)
    right = dot(cross, inverse, 1, 1, HIGH)
    ortho = dot(left, inverse, 1, 1, HIGH)
    squares = lax.psum(jnp.sum(right * right, axis=0), "tp")
    new_momentum = mixed - 0.05 * dot(ortho, right, 1, 1, lax.Precision.DEFAULT)
    colnorm = jnp.sqrt(squares + 1e-08)
    new_basis = dot(cross_mine, inverse, 1, 1, HIGH) / colnorm
    factor = jnp.sqrt(jnp.float32(M) * jnp.float32(N) / jnp.float32(RANK))
    update = dot(factor * ortho / colnorm, right, 1, 1, HIGH).astype(jnp.bfloat16)
    return (new_momentum, new_basis, update)


def solution(mesh):
    placed = (P("fsdp", "tp"), P("fsdp", "tp"), P(("tp", "fsdp"), None))
    return jax.shard_map(
        local,
        mesh=mesh,
        in_specs=placed,
        out_specs=(P("fsdp", "tp"), P(("tp", "fsdp"), None), P("fsdp", "tp")),
        check_vma=False,
    )
```

time: 888 us -> 502 us (0.57)
  other arithmetic: 269 us -> 0.01 us
  matrix products: 165 us -> 66.3 us
  Pallas kernels: 0 us -> 72.8 us
  blocking collectives: 66.6 us -> 12 us
  local copies, waits for them, and re-layouts: 37 us -> 4.16 us
  waiting for transfers between devices: 323 us -> 332 us
    another operation x33 -> x0, other arithmetic: 256 us -> none  [the longest x30 173 us: local(): lower = jnp.linalg.cholesky(gram)]
    pallas_call x0 -> x1, Pallas kernels: none -> 72.8 us  [cholesky_inverse(): pl.pallas_call(inverse_kernel, out_shape=jax.ShapeDtypeStruct(gram.shape,...]
    psum x1, blocking collectives: 66.6 us -> 12 us  [local(): squares = lax.psum(jnp.sum(right * right, axis=0), 'tp')]
    dot_general x4 -> x8, matrix products: 119 us -> 66.3 us  [dot(): lax.dot_general(a, b, dims, precision=precision, preferred_element_type=j...]
    another operation x29 -> x0, matrix products: 46.2 us -> none  [the longest x15 23.2 us: local(): lax.linalg.triangular_solve(lower, left, left_side=False, lower=True, tra...]
    all_gather x1 -> x2, waiting for transfers between devices: 0.01 us -> 34.5 us  [the longest x1 34.5 us: local(): lax.all_gather(lax.psum(gram_part.T, 'fsdp'), 'tp', axis=0, tiled=True)]
    psum x2, waiting for transfers between devices: 168 us -> 139 us  [the longest x1 75.4 us: local(): lax.psum(gram_part.T, 'fsdp')]
    another operation x33 -> x0, local copies, waits for them, and re-layouts: 25.6 us -> none
  transfers between devices with their start and end apart: 5 -> 6, of which waited for: 4 -> 5; matrix products, arithmetic and copies ran while one was open for 1% -> 3% of each run, Pallas kernels for 0% -> 15%
where the time goes in v1:
time: 502 us
  waiting for transfers between devices  332 us (66%)
  Pallas kernels  72.8 us (15%)
  matrix products  66.3 us (13%)
  between operations  14.2 us (3%)
  blocking collectives  12 us (2%)
    reduce_scatter x1, waiting for transfers between devices, local(): lax.psum_scatter(dot(mixed, left, 0, 0, HIGH), 'fsdp', scatter_dimension=...  86.1 us
    psum x1, waiting for transfers between devices, local(): lax.psum(gram_part.T, 'fsdp')  75.4 us
    pallas_call x1, Pallas kernels, cholesky_inverse(): pl.pallas_call(inverse_kernel, out_shape=jax.ShapeDtypeStruct(gram.shape,...  72.8 us
    all_gather x1, waiting for transfers between devices, local(): lax.all_gather(basis, 'fsdp', axis=0, tiled=True)  71.7 us
    dot_general x8, matrix products, dot(): lax.dot_general(a, b, dims, precision=precision, preferred_element_type=j...  66.3 us
    psum x1, waiting for transfers between devices, local(): lax.psum(dot(mixed, lax.all_gather(basis, 'fsdp', axis=0, tiled=True), 1,...  63.4 us
    all_gather x1, waiting for transfers between devices, local(): lax.all_gather(lax.psum(gram_part.T, 'fsdp'), 'tp', axis=0, tiled=True)  34.5 us
    psum x1, blocking collectives, local(): squares = lax.psum(jnp.sum(right * right, axis=0), 'tp')  12 us
  transfers between devices with their start and end apart: 6, of which 5 were waited for; matrix products, arithmetic and copies ran while one was open for 3% of the time, Pallas kernels for 15%

profile of v1, /device:TPU:1, one launch (start us, length us, event | category | flops | bytes accessed | tf_op | source)
XLA Modules:
  0.0 501.7 jit_solution(369293747123003025)
XLA Ops:
  7.2 0.0 all-gather.4.cloned.1.call-start
  7.2 0.7 all-gather.4.cloned.1.call-update
  7.9 0.0 all-reduce.3.cloned.1.call-start
  7.9 71.7 %all-gather.4.cloned.1.call-done = f32[1792,1024]{1,0:T(8,128)} async-done(((f32[112,1024]{1,0:T(8,128)}), f32[1792,1024]{1,0:T(8,128)}) %all-gather.4.cloned.1.call-update) | async-done | bytes 7340048 | tf_op jit(solution)/shard_map/all_gather | solution.py:111
  79.7 10.8 %fusion.3 = f32[512,1024]{1,0:T(8,128)} fusion(f32[1792,1024]{1,0:T(8,128)} %all-gather.4.cloned.1.call-done, f32[512,1792]{1,0:T(8,128)} %param.4, bf16[512,1792]{1,0:T(8,128)(2,1)} %param.3), kind=kOutput, calls=%fused_computation.7 | convolution fusion | flops 5638979584 | bytes 14942208 | tf_op jit(solution)/shard_map/dot_general | solution.py:21
  90.6 0.0 all-reduce.5.cloned.1.call-start
  90.6 63.4 %all-reduce.3.cloned.1.call-done = f32[512,1024]{1,0:T(8,128)} async-done(((f32[512,1024]{1,0:T(8,128)}), f32[512,1024]{1,0:T(8,128)}) %all-reduce.3.cloned.1.call-update) | async-done | bytes 2097168 | tf_op jit(solution)/shard_map/psum | solution.py:111
  154.0 3.8 fusion.6
  157.8 0.0 reduce-scatter.2.cloned.1.call-start
  157.9 10.2 %fusion.2 = f32[1792,1024]{1,0:T(8,128)} fusion(f32[512,1024]{1,0:T(8,128)} %all-reduce.3.cloned.1.call-done, f32[512,1792]{1,0:T(8,128)} %param.4, bf16[512,1792]{1,0:T(8,128)(2,1)S(1)} %copy-done.3), kind=kOutput, calls=%fused_computation.6 | convolution fusion | flops 5638979584 | bytes 14942208 | tf_op jit(solution)/shard_map/dot_general | solution.py:21
  168.1 0.0 all-gather.6.cloned.1.call-start
  168.1 75.4 %all-reduce.5.cloned.1.call-done = f32[128,1024]{1,0:T(8,128)} async-done(((f32[128,1024]{1,0:T(8,128)}), f32[128,1024]{1,0:T(8,128)}) %all-reduce.5.cloned.1.call-update) | async-done | bytes 524304 | tf_op jit(solution)/shard_map/psum | solution.py:114
  243.5 0.2 all-gather.8.cloned.1.call-start
  243.8 86.1 %reduce-scatter.2.cloned.1.call-done = f32[112,1024]{1,0:T(8,128)} async-done(((f32[1792,1024]{1,0:T(8,128)}), f32[112,1024]{1,0:T(8,128)}) %reduce-scatter.2.cloned.1.call-update) | async-done | bytes 458768 | tf_op jit(solution)/shard_map/reduce_scatter | solution.py:115
  329.9 34.5 %all-gather.6.cloned.1.call-done.gram_ref = f32[1024,1024]{1,0:T(8,128)} async-done(((f32[128,1024]{1,0:T(8,128)}), f32[1024,1024]{1,0:T(8,128)}) %all-gather.6.cloned.1.call-update) | async-done | bytes 4194320 | tf_op jit(solution)/shard_map/all_gather | solution.py:114
  364.4 2.2 copy-done.2
  366.6 72.8 %cholesky_inverse.1 = f32[1024,1024]{1,0:T(8,128)S(1)} custom-call(f32[1024,1024]{1,0:T(8,128)S(1)} %copy-done.2), custom_call_target="tpu_custom_call" | custom-call | flops 60000002048 | bytes 8388608 | tf_op jit(solution)/shard_map/cholesky_inverse/pallas_call | solution.py:97
  439.4 1.9 copy-done
  441.4 4.8 fusion.10
  446.2 16.6 %multiply_reduce_fusion = (f32[1024]{0:T(1024)S(1)}, f32[1792,1024]{1,0:T(8,128)}) fusion(f32[1792,1024]{1,0:T(8,128)} %all-gather.8.cloned.1.call-done, f32[1024,1024]{1,0:T(8,128)} %copy-done), kind=kOutput, calls=%fused_computation | convolution fusion | flops 11277958144 | bytes 18878464 | tf_op jit(solution)/shard_map/dot_general | solution.py:21
  462.8 12.0 %psum.23 = f32[1024]{0:T(1024)S(1)} all-reduce(f32[1024]{0:T(1024)S(1)} %get-tuple-element.3), channel_id=1, replica_groups=mesh['fsdp'=16,'tp'=8] {'tp'}, use_global_device_ids=true, to_apply=%region_4.0 | all-reduce | flops 1024 | bytes 8192 | tf_op jit(solution)/shard_map/psum | solution.py:120
  474.8 8.8 %multiply_subtract_fusion = f32[512,1792]{1,0:T(8,128)} fusion(f32[512,1024]{1,0:T(8,128)} %fusion.10, f32[1792,1024]{1,0:T(8,128)} %get-tuple-element.4, f32[512,1792]{1,0:T(8,128)} %param.4, bf16[512,1792]{1,0:T(8,128)(2,1)S(1)} %copy-done.3), kind=kOutput, calls=%fused_computation.1 | convolution fusion | flops 1882718208 | bytes 18612224 | tf_op jit(solution)/shard_map/dot_general | solution.py:21
  483.7 8.2 %convolution_convert_fusion = bf16[512,1792]{1,0:T(8,128)(2,1)} fusion(f32[1792,1024]{1,0:T(8,128)S(1)} %copy-done.6, f32[512,1024]{1,0:T(8,128)S(1)} %copy-done.5, f32[1024]{0:T(1024)S(1)} %add_sqrt_fusion), kind=kOutput, calls=%fused_computation.3 | convolution fusion | flops 5639110656 | bytes 11276288 | tf_op jit(solution)/shard_map/dot_general | solution.py:21
  491.9 3.0 convolution_divide_fusion
  (21 shorter events, 0.1 us)
Async XLA Ops:
  7.2 72.5 %all-gather.4.cloned.1.call-start = ((), (), s32[]{:S(2)}) async-start(), calls=%async_computation.1 | async-start | bytes 7798784 | tf_op jit(solution)/shard_map/all_gather | solution.py:111
  7.9 146.1 %all-reduce.3.cloned.1.call-start = ((), (), s32[]{:S(2)}) async-start(), calls=%async_computation.2 | async-start | bytes 4194304 | tf_op jit(solution)/shard_map/psum | solution.py:111
  90.5 67.3 %copy-start.3 = (bf16[512,1792]{1,0:T(8,128)(2,1)S(1)}, bf16[512,1792]{1,0:T(8,128)(2,1)}, u32[]{:S(2)}) copy-start(bf16[512,1792]{1,0:T(8,128)(2,1)} %param.3) | copy-start | bytes 5505028
  90.6 153.0 %all-reduce.5.cloned.1.call-start = ((), (), s32[]{:S(2)}) async-start(), calls=%async_computation.3 | async-start | bytes 1048576 | tf_op jit(solution)/shard_map/psum | solution.py:114
  157.8 172.1 %reduce-scatter.2.cloned.1.call-start = ((), (), s32[]{:S(2)}) async-start(), calls=%async_computation.5 | async-start | bytes 7798784 | tf_op jit(solution)/shard_map/reduce_scatter | solution.py:115
  168.1 196.3 %all-gather.6.cloned.1.call-start = ((), (), s32[]{:S(2)}) async-start(), calls=%async_computation.4 | async-start | bytes 4718592 | tf_op jit(solution)/shard_map/all_gather | solution.py:114
  243.5 202.6 %all-gather.8.cloned.1.call-start = ((), (), s32[]{:S(2)}) async-start(), calls=%async_computation.6 | async-start | bytes 7798784 | tf_op jit(solution)/shard_map/all_gather | solution.py:116
  364.4 2.2 copy-start.2
  366.6 74.8 %copy-start.4 = (f32[512,1024]{1,0:T(8,128)S(1)}, f32[512,1024]{1,0:T(8,128)}, u32[]{:S(2)}) copy-start(f32[512,1024]{1,0:T(8,128)} %all-reduce.3.cloned.1.call-done) | copy-start | bytes 6291460
  439.4 2.0 copy-start
  474.8 8.9 %copy-start.5 = (f32[512,1024]{1,0:T(8,128)S(1)}, f32[512,1024]{1,0:T(8,128)}, u32[]{:S(2)}) copy-start(f32[512,1024]{1,0:T(8,128)} %fusion.10) | copy-start | bytes 6291460
  474.8 8.9 %copy-start.6 = (f32[1792,1024]{1,0:T(8,128)S(1)}, f32[1792,1024]{1,0:T(8,128)}, u32[]{:S(2)}) copy-start(f32[1792,1024]{1,0:T(8,128)} %get-tuple-element.4) | copy-start | bytes 22020100
  483.7 8.2 %copy-start.1 = (f32[1024,1024]{1,0:T(8,128)S(1)}, f32[1024,1024]{1,0:T(8,128)}, u32[]{:S(2)}) copy-start(f32[1024,1024]{1,0:T(8,128)} %copy-done) | copy-start | bytes 12582916
  483.7 8.2 %copy-start.7 = (f32[112,1024]{1,0:T(8,128)S(1)}, f32[112,1024]{1,0:T(8,128)}, u32[]{:S(2)}) copy-start(f32[112,1024]{1,0:T(8,128)} %reduce-scatter.2.cloned.1.call-done) | copy-start | bytes 1376260
Sparse Core Ops, SparseCore 0:
  10.2 69.4 all-gather.3
  90.7 63.2 all-reduce.2
  157.9 85.5 all-reduce.4
  247.3 82.6 reduce-scatter.1
  331.5 32.8 all-gather.5
  366.4 65.9 all-gather.7

commit v2 on v1

--- a/solution.py
+++ b/solution.py
@@ -14,6 +14,10 @@
 STRIP = 8
 HIGHEST = lax.Precision.HIGHEST
 HIGH = lax.Precision.HIGH
+MESH = pl.DeviceIdType.MESH
+SHARD = 112
+HALF = 56
+WIDE = 512
 
 
 def dot(a, b, ca, cb, precision):
@@ -27,7 +31,7 @@
     return r * (2.0 - d * r)
 
 
-def factor(block):
+def factor(block, pause):
     shape = (STRIP, BLOCK)
     lane = lax.broadcasted_iota(jnp.int32, shape, 1)
     sub = lax.broadcasted_iota(jnp.int32, shape, 0)
@@ -35,6 +39,8 @@
     strips = [block[STRIP * t : STRIP * (t + 1), :] for t in range(count)]
     out = []
     for s in range(count):
+        if s in (4, 8, 12):
+            pause()
         first = STRIP * s
         w = strips[s]
         columns = [jnp.broadcast_to(w[:, first + j : first + j + 1], shape) for j in range(STRIP)]
@@ -67,19 +73,378 @@
     return jnp.concatenate(out, axis=0)
 
 
-def inverse_kernel(gram_ref, out_ref, held):
+def split(x):
+    high = x.astype(jnp.bfloat16)
+    return high, (x - high.astype(jnp.float32)).astype(jnp.bfloat16)
+
+
+def dot3(ah, al, bh, bl, ca, cb):
+    def one(a, b):
+        dims = (((ca,), (cb,)), ((), ()))
+        return lax.dot_general(a, b, dims, preferred_element_type=jnp.float32)
+
+    return one(ah, bh) + (one(ah, bl) + one(al, bh))
+
+
+class Net:
+    def __init__(self, send_sem, recv_sem):
+        self.send_sem, self.recv_sem, self.made, self.open = send_sem, recv_sem, {}, []
+        self.index, self.dry = {}, False
+        fsdp, tp = lax.axis_index("fsdp"), lax.axis_index("tp")
+        self.y, self.z = fsdp // 4, fsdp % 4
+        self.x, self.core = tp // 2, tp % 2
+
+    def at(self, y=0, z=0, x=0, core=0):
+        f = ((self.y + y + 4) % 4) * 4 + (self.z + z + 4) % 4
+        t = ((self.x + x + 4) % 4) * 2 + (self.core + core) % 2
+        return (f, t)
+
+    def send(self, key, source, target, to):
+        i = self.index.setdefault(key, len(self.index))
+
+        def make():
+            return pltpu.make_async_remote_copy(
+                src_ref=source(),
+                dst_ref=target(),
+                send_sem=self.send_sem.at[i],
+                recv_sem=self.recv_sem.at[i],
+                device_id=self.at(**to),
+                device_id_type=MESH,
+            )
+
+        self.made[key] = make
+        if not self.dry:
+            self.open.append(key)
+            make().start()
+
+    def got(self, *keys):
+        for key in () if self.dry else keys:
+            self.made[key]().wait_recv()
+
+    def sent(self, name=None):
+        done = [key for key in self.open if name is None or key[0] == name]
+        for key in done:
+            self.made[key]().wait_send()
+        self.open = [key for key in self.open if key not in done]
+
+
+def shard_of(net, ref, first, o1, o2, half, part):
+    dy, dz = (o1, o2) if first == "y" else (o2, o1)
+    index = ((net.y + dy + 4) % 4) * 4 + (net.z + dz + 4) % 4
+    at, rows = {"all": (0, SHARD), "top": (0, HALF), "low": (HALF, HALF)}[part]
+    return ref.at[pl.ds(pl.multiple_of(index * SHARD + at, 8), rows), pl.ds(half * WIDE, WIDE)]
+
+
+def gather_events(net, name, own, buf):
+    lists = []
+    for half, (d1, d2) in enumerate((("y", "z"), ("z", "y"))):
+        key = lambda *k, half=half: (name, half) + k
+        shard = lambda o1, o2, part="all", d1=d1, half=half: shard_of(net, buf, d1, o1, o2, half, part)
+
+        def both(o, key=key, shard=shard, d2=d2):
+            for way, sign in ((1, "+"), (-1, "-")):
+                net.send(key(2, o, sign), lambda: shard(o, 0), lambda: shard(o, 0), {d2: way})
+
+        def start(key=key, shard=shard, d1=d1, d2=d2, half=half):
+            mine = lambda: own(half)
+            for way, sign in ((1, "+"), (-1, "-")):
+                net.send(key(1, sign), mine, lambda: shard(0, 0), {d1: way})
+            for way, sign in ((1, "+"), (-1, "-")):
+                net.send(key(2, 0, sign), mine, lambda: shard(0, 0), {d2: way})
+
+        def near(o, way, sign, part, key=key, shard=shard, d1=d1, both=both):
+            net.got(key(1, sign))
+            net.send(key(1, "f" + sign), lambda: shard(o, 0, part), lambda: shard(o, 0, part), {d1: way})
+            both(o)
+
+        def far(key=key, both=both):
+            net.got(key(1, "f+"), key(1, "f-"))
+            both(2)
+
+        def pass_on(o, p, way, sign, part, key=key, shard=shard, d2=d2):
+            net.got(key(2, o, sign))
+            net.send(key(2, o, "f" + sign), lambda: shard(o, p, part), lambda: shard(o, p, part), {d2: way})
+
+        def last(key=key):
+            for o in (0, -1, 1, 2):
+                net.got(key(2, o, "f+"), key(2, o, "f-"))
+
+        events = [start, functools.partial(near, -1, 1, "+", "top"), functools.partial(near, 1, -1, "-", "low")]
+        for i, o in enumerate((0, -1, 1, 2)):
+            if i == 1:
+                events.append(far)
+            events.append(functools.partial(pass_on, o, -1, 1, "+", "top"))
+            events.append(functools.partial(pass_on, o, 1, -1, "-", "low"))
+        events.append(last)
+        lists.append(events)
+    return [e for pair in zip(*lists) for e in pair]
+
+
+def scatter_events(net, name, buf, ra, rb, rc, rd):
+    lists = []
+    order = (2, 1, -1, 0)
+    for half, (e1, e2) in enumerate((("y", "z"), ("z", "y"))):
+        key = lambda *k, half=half: (name, half) + k
+        shard = lambda o1, o2, part="all", e1=e1, half=half: shard_of(net, buf, e1, o1, o2, half, part)
+
+        def add(ref, *others):
+            if net.dry:
+                return
+            total = ref[...]
+            for other in others:
+                total = total + other[...]
+            ref[...] = total
+
+        def start(o, key=key, shard=shard, e1=e1, half=half):
+            i = (half * 4 + order.index(o)) * 2
+            net.send(key(1, o, "f+"), lambda: shard(2, o, "top"), lambda: ra.at[i], {e1: 1})
+            net.send(key(1, o, "f-"), lambda: shard(2, o, "low"), lambda: ra.at[i + 1], {e1: -1})
+
+        def near(o, way, sign, part, j, key=key, shard=shard, e1=e1, half=half):
+            i = (half * 4 + order.index(o)) * 2 + j
+            net.got(key(1, o, "f" + sign))
+            add(shard(way, o, part), ra.at[i])
+            net.send(key(1, o, sign), lambda: shard(way, o), lambda: rb.at[i], {e1: way})
+
+        def line(o, key=key, shard=shard, half=half):
+            i = (half * 4 + order.index(o)) * 2
+            net.got(key(1, o, "+"), key(1, o, "-"))
+            add(shard(0, o), rb.at[i], rb.at[i + 1])
+
+        def far(key=key, shard=shard, e2=e2, half=half, line=line):
+            line(2)
+            net.send(key(2, "f+"), lambda: shard(0, 2, "top"), lambda: rc.at[2 * half], {e2: 1})
+            net.send(key(2, "f-"), lambda: shard(0, 2, "low"), lambda: rc.at[2 * half + 1], {e2: -1})
+
+        def side(way, sign, part, j, key=key, shard=shard, e2=e2, half=half, line=line):
+            line(way)
+            net.got(key(2, "f" + sign))
+            add(shard(0, way, part), rc.at[2 * half + j])
+            net.send(key(2, sign), lambda: shard(0, way), lambda: rd.at[2 * half + j], {e2: way})
+
+        def mine(key=key, shard=shard, half=half, line=line):
+            line(0)
+            net.got(key(2, "+"), key(2, "-"))
+            add(shard(0, 0), rd.at[2 * half], rd.at[2 * half + 1])
+
+        events = [functools.partial(start, o) for o in order]
+        for o in order:
+            events.append(functools.partial(near, o, 1, "+", "top", 0))
+            events.append(functools.partial(near, o, -1, "-", "low", 1))
+            if o == 1:
+                events.append(far)
+        events.append(functools.partial(side, 1, "+", "top", 0))
+        events.append(functools.partial(side, -1, "-", "low", 1))
+        events.append(mine)
+        lists.append(events)
+    return [e for pair in zip(*lists) for e in pair]
+
+
+def tp_gather_events(net, name, ref, piece, start_of):
+    def part(dx, which="all"):
+        at, rows = {"all": (0, piece), "top": (0, piece // 2), "low": (piece // 2, piece // 2)}[which]
+        return ref.at[pl.ds(pl.multiple_of(start_of(dx) + at, 8), rows), :]
+
+    def put(key, dx, which, to):
+        net.send((name,) + key, lambda: part(dx, which), lambda: part(dx, which), to)
+
+    def start():
+        put(("+",), 0, "all", {"x": 1})
+        put(("-",), 0, "all", {"x": -1})
+        put(("c", 0), 0, "all", {"core": 1})
+
+    def near():
+        net.got((name, "+"))
+        put(("f+",), -1, "top", {"x": 1})
+        net.got((name, "-"))
+        put(("f-",), 1, "low", {"x": -1})
+        put(("c", -1), -1, "all", {"core": 1})
+        put(("c", 1), 1, "all", {"core": 1})
+
+    def last():
+        net.got((name, "f+"), (name, "f-"))
+        put(("c", 2), 2, "all", {"core": 1})
+        net.got(*[(name, "c", dx) for dx in (0, -1, 1, 2)])
+
+    return start, near, last
+
+
+def tp_sum(net, ref, out, lc, la, lb):
+    mine = net.core * 256
+    other = 256 - mine
+    net.send(("core",), lambda: ref.at[pl.ds(pl.multiple_of(other, 8), 256), :], lambda: lc, {"core": 1})
+    net.got(("core",))
+    rows = pl.ds(pl.multiple_of(mine, 8), 256)
+    ref[rows, :] = ref[rows, :] + lc[...]
+
+    def start_of(dx):
+        return mine + ((net.x + dx + 4) % 4) * 64
+
+    def piece(dx, at=0, count=64):
+        return ref.at[pl.ds(pl.multiple_of(start_of(dx) + at, 8), count), :]
+
+    net.send(("xf+",), lambda: piece(2, 0, 32), lambda: la.at[0], {"x": 1})
+    net.send(("xf-",), lambda: piece(2, 32, 32), lambda: la.at[1], {"x": -1})
+    for way, sign, at, j in ((1, "+", 0, 0), (-1, "-", 32, 1)):
+        net.got(("xf" + sign,))
+        there = piece(way, at, 32)
+        there[...] = there[...] + la[j]
+        net.send(("x" + sign,), lambda way=way: piece(way), lambda j=j: lb.at[j], {"x": way})
+    net.got(("x+",), ("x-",))
+    out[pl.ds(pl.multiple_of(start_of(0), 8), 64), :] = piece(0)[...] + lb[0] + lb[1]
+    for event in tp_gather_events(net, "left", out, 64, start_of):
+        event()
+
+
+def main_kernel(
+    momentum_ref, gradient_ref, basis_ref, left_ref, cross_ref, inverse_ref,
+    buf, mh, ml, lbuf, lc, la, lb, lh, ll, ra, rb, rc, rd, held, gpart, gsum, send_sem, recv_sem,
+):
+    net = Net(send_sem, recv_sem)
+    me = net.y * 4 + net.z
+    tp = net.x * 2 + net.core
+    barrier = pltpu.get_barrier_semaphore()
+    for i in range(1, 16):
+        pl.semaphore_signal(barrier, inc=1, device_id=((me + i) % 16, tp), device_id_type=MESH)
+    near = ({"x": 1}, {"x": -1}, {"core": 1})
+    for to in near:
+        pl.semaphore_signal(barrier, inc=1, device_id=net.at(**to), device_id_type=MESH)
+    pl.semaphore_wait(barrier, 15 + len(near))
+
+    events = gather_events(net, "basis", lambda half: basis_ref.at[:, pl.ds(half * WIDE, WIDE)], buf)
+    for event in events[:2]:
+        event()
+    buf[pl.ds(pl.multiple_of(me * SHARD, 8), SHARD), :] = basis_ref[...]
+
+    @pl.loop(0, 16)
+    def _(i):
+        rows = pl.ds(pl.multiple_of(i * 32, 32), 32)
+        mh[rows, :], ml[rows, :] = split(momentum_ref[rows, :] + gradient_ref[rows, :].astype(jnp.float32))
+
+    for event in events[2:]:
+        event()
+
+    @pl.loop(0, 4)
+    def _(i):
+        columns = pl.ds(pl.multiple_of(i * 256, 256), 256)
+        bh, bl = split(buf[:, columns])
+        lbuf[:, columns] = dot3(mh[...], ml[...], bh, bl, 1, 0)
+
+    tp_sum(net, lbuf, left_ref, lc, la, lb)
+    net.sent()
+
+    own_rows = pl.ds(pl.multiple_of(tp * BLOCK, BLOCK), BLOCK)
+    gpart[...] = dot(left_ref[:, own_rows], left_ref[...], 0, 0, HIGHEST)
+    copies = []
+    for i in range(1, 16):
+        to = (me + i) % 16
+        copies.append(
+            pltpu.make_async_remote_copy(
+                src_ref=gpart.at[pl.ds(pl.multiple_of(to * 8, 8), 8), :],
+                dst_ref=gsum.at[i],
+                send_sem=send_sem.at[150 + i],
+                recv_sem=recv_sem.at[150 + i],
+                device_id=(to, tp),
+                device_id_type=MESH,
+            )
+        )
+        copies[-1].start()
+
+    lh[...], ll[...] = split(left_ref[...])
+
+    @pl.loop(0, 7)
+    def _(i):
+        columns = pl.ds(pl.multiple_of(i * 256, 256), 256)
+        buf[columns, :] = dot3(mh[:, columns], ml[:, columns], lh[...], ll[...], 0, 0)
+
+    scatter = scatter_events(net, "scatter", buf, ra, rb, rc, rd)
+    for event in scatter[:8]:
+        event()
+    for copy in copies:
+        copy.wait()
+    total = gpart[pl.ds(pl.multiple_of(me * 8, 8), 8), :]
+    for i in range(1, 16):
+        total = total + gsum[i]
+    at = pl.multiple_of(tp * BLOCK + me * 8, 8)
+    held[pl.ds(at, 8), :] = total
+    copies = []
+    for i in range(1, 16):
+        copies.append(
+            pltpu.make_async_remote_copy(
+                src_ref=held.at[pl.ds(at, 8), :],
+                dst_ref=held.at[pl.ds(at, 8), :],
+                send_sem=send_sem.at[170 + i],
+                recv_sem=recv_sem.at[170 + i],
+                device_id=((me + i) % 16, tp),
+                device_id_type=MESH,
+            )
+        )
+        copies[-1].start()
+    for event in scatter[8:12]:
+        event()
+    for copy in copies:
+        copy.wait()
+    gram_events = tp_gather_events(
+        net, "gram", held, BLOCK, lambda dx: (((net.x + dx + 4) % 4) * 2 + net.core) * BLOCK
+    )
+    gram_events[0]()
+    for event in scatter[12:18]:
+        event()
+    gram_events[1]()
+    for event in scatter[18:22]:
+        event()
+    gram_events[2]()
+    net.sent("gram")
+
+    def own(half):
+        return shard_of(net, buf, "y", 0, 0, half, "all")
+
+    def keep():
+        if net.dry:
+            return
+        rows = pl.ds(pl.multiple_of(me * SHARD, 8), SHARD)
+        cross_ref[rows, :] = buf[rows, :]
+
+    rest = scatter[22:] + [keep] + gather_events(net, "cross", own, cross_ref)
+    eliminate(net, held, inverse_ref, rest)
+    net.sent()
+
+
+def eliminate(net, held, out_ref, events):
     n = held.shape[0]
-    held[...] = gram_ref[...]
+    count = n // BLOCK
     shape = (BLOCK, BLOCK)
     eye = (lax.broadcasted_iota(jnp.int32, shape, 0) == lax.broadcasted_iota(jnp.int32, shape, 1)).astype(jnp.float32)
     lanes = lax.broadcasted_iota(jnp.int32, (BLOCK, n), 1)
+    slots = 5 * count
+    plan = [events[len(events) * i // slots : len(events) * (i + 1) // slots] for i in range(slots)]
+    net.dry = True
+    for event in events:
+        event()
+    net.dry = False
 
     def step(k, carry):
+        used = []
+
+        def pause():
+            for i in range(count):
+                group = plan[5 * i + len(used)]
+                if group:
+
+                    @pl.when(k == i)
+                    def _():
+                        for event in group:
+                            event()
+
+            used.append(None)
+
         mine = pl.ds(pl.multiple_of(k * BLOCK, BLOCK), BLOCK)
-        inverse = factor(held[mine, mine])
+        pause()
+        inverse = factor(held[mine, mine], pause)
         held[mine, mine] = eye
         held[mine, :] = dot(inverse, held[mine, :], 1, 0, HIGHEST)
         out_ref[mine, :] = jnp.where(lanes < (k + 1) * BLOCK, held[mine, :], 0.0)
+        pause()
 
         def below(t, inner):
             rows = pl.ds(pl.multiple_of(t * BLOCK, BLOCK), BLOCK)
@@ -87,42 +452,65 @@
             held[rows, :] = held[rows, :] - dot(held[mine, rows], held[mine, :], 0, 0, HIGHEST)
             return inner
 
-        lax.fori_loop(k + 1, n // BLOCK, below, 0)
+        lax.fori_loop(k + 1, count, below, 0)
         return carry
 
-    lax.fori_loop(0, n // BLOCK, step, 0)
-
-
-def cholesky_inverse(gram):
+    lax.fori_loop(0, count, step, 0)
+
+
+def factors(momentum, gradient, basis):
+    f32, bf16 = jnp.float32, jnp.bfloat16
+    rows, columns = momentum.shape
+    vmem = pl.BlockSpec(memory_space=pltpu.VMEM)
     return pl.pallas_call(
-        inverse_kernel,
-        out_shape=jax.ShapeDtypeStruct(gram.shape, jnp.float32),
-        in_specs=[pl.BlockSpec(memory_space=pltpu.VMEM)],
-        out_specs=pl.BlockSpec(memory_space=pltpu.VMEM),
-        scratch_shapes=[pltpu.VMEM(gram.shape, jnp.float32)],
-        compiler_params=pltpu.CompilerParams(vmem_limit_bytes=32 << 20),
-        cost_estimate=pl.CostEstimate(flops=60_000_000_000, bytes_accessed=8 << 20, transcendentals=0),
-        name="cholesky_inverse",
-    )(gram)
+        main_kernel,
+        out_shape=[
+            jax.ShapeDtypeStruct((rows, RANK), f32),
+            jax.ShapeDtypeStruct((columns, RANK), f32),
+            jax.ShapeDtypeStruct((RANK, RANK), f32),
+        ],
+        in_specs=[vmem] * 3,
+        out_specs=[vmem] * 3,
+        scratch_shapes=[
+            pltpu.VMEM((columns, RANK), f32),
+            pltpu.VMEM((rows, columns), bf16),
+            pltpu.VMEM((rows, columns), bf16),
+            pltpu.VMEM((rows, RANK), f32),
+            pltpu.VMEM((256, RANK), f32),
+            pltpu.VMEM((2, 32, RANK), f32),
+            pltpu.VMEM((2, 64, RANK), f32),
+            pltpu.VMEM((rows, RANK), bf16),
+            pltpu.VMEM((rows, RANK), bf16),
+            pltpu.VMEM((16, HALF, WIDE), f32),
+            pltpu.VMEM((16, SHARD, WIDE), f32),
+            pltpu.VMEM((4, HALF, WIDE), f32),
+            pltpu.VMEM((4, SHARD, WIDE), f32),
+            pltpu.VMEM((RANK, RANK), f32),
+            pltpu.VMEM((BLOCK, RANK), f32),
+            pltpu.VMEM((16, 8, RANK), f32),
+            pltpu.SemaphoreType.DMA((192,)),
+            pltpu.SemaphoreType.DMA((192,)),
+        ],
+        compiler_params=pltpu.CompilerParams(
+            collective_id=0, has_side_effects=True, vmem_limit_bytes=62 << 20
+        ),
+        cost_estimate=pl.CostEstimate(flops=60_000_000_000, bytes_accessed=30 << 20, transcendentals=0),
+        name="factors",
+    )(momentum, gradient, basis)
 
 
 def local(gradient, momentum, basis):
     mixed = momentum + gradient.astype(jnp.float32)
-    left = lax.psum(dot(mixed, lax.all_gather(basis, "fsdp", axis=0, tiled=True), 1, 0, HIGH), "tp")
-    part = lax.axis_index("tp") * BLOCK
-    gram_part = dot(left, lax.dynamic_slice_in_dim(left, part, BLOCK, 1), 0, 0, HIGHEST)
-    gram = lax.all_gather(lax.psum(gram_part.T, "fsdp"), "tp", axis=0, tiled=True)
-    cross_mine = lax.psum_scatter(dot(mixed, left, 0, 0, HIGH), "fsdp", scatter_dimension=0, tiled=True)
-    cross = lax.all_gather(cross_mine, "fsdp", axis=0, tiled=True)
-    inverse = cholesky_inverse(gram)
+    left, cross, inverse = factors(momentum, gradient, basis)
     right = dot(cross, inverse, 1, 1, HIGH)
     ortho = dot(left, inverse, 1, 1, HIGH)
     squares = lax.psum(jnp.sum(right * right, axis=0), "tp")
     new_momentum = mixed - 0.05 * dot(ortho, right, 1, 1, lax.Precision.DEFAULT)
     colnorm = jnp.sqrt(squares + 1e-08)
-    new_basis = dot(cross_mine, inverse, 1, 1, HIGH) / colnorm
-    factor = jnp.sqrt(jnp.float32(M) * jnp.float32(N) / jnp.float32(RANK))
-    update = dot(factor * ortho / colnorm, right, 1, 1, HIGH).astype(jnp.bfloat16)
+    first = lax.axis_index("fsdp") * SHARD
+    new_basis = lax.dynamic_slice_in_dim(right, first, SHARD, 0) / colnorm
+    scale = jnp.sqrt(jnp.float32(M) * jnp.float32(N) / jnp.float32(RANK))
+    update = dot(scale * ortho / colnorm, right, 1, 1, HIGH).astype(jnp.bfloat16)
     return (new_momentum, new_basis, update)
 
 

time: 502 us -> 284 us (0.57)
  waiting for transfers between devices: 332 us -> 0 us
  Pallas kernels: 72.8 us -> 229 us
  matrix products: 66.3 us -> 35.7 us
  between operations: 14.2 us -> 0.7 us
    pallas_call x1, Pallas kernels: 72.8 us -> 229 us  [factors(): pl.pallas_call(main_kernel, out_shape=[jax.ShapeDtypeStruct((rows, RANK),...]
    psum x2 -> x0, waiting for transfers between devices: 139 us -> none  [the longest x1 75.4 us: local(): lax.psum(gram_part.T, 'fsdp')]
    all_gather x3 -> x0, waiting for transfers between devices: 106 us -> none  [the longest x1 71.7 us: local(): lax.all_gather(basis, 'fsdp', axis=0, tiled=True)]
    reduce_scatter x1 -> x0, waiting for transfers between devices: 86.1 us -> none  [local(): lax.psum_scatter(dot(mixed, left, 0, 0, HIGH), 'fsdp', scatter_dimension=...]
    dot_general x8 -> x4, matrix products: 66.3 us -> 35.7 us  [dot(): lax.dot_general(a, b, dims, precision=precision, preferred_element_type=j...]
  transfers between devices with their start and end apart: 6 -> 0, of which waited for: 5 -> 0; matrix products, arithmetic and copies ran while one was open for 3% -> 0% of each run, Pallas kernels for 15% -> 0%
where the time goes in v2:
time: 284 us
  Pallas kernels  229 us (81%)
  matrix products  35.7 us (13%)
  blocking collectives  14.2 us (5%)
  local copies, waits for them, and re-layouts  2.97 us (1%)
    pallas_call x1, Pallas kernels, factors(): pl.pallas_call(main_kernel, out_shape=[jax.ShapeDtypeStruct((rows, RANK),...  229 us
    dot_general x4, matrix products, dot(): lax.dot_general(a, b, dims, precision=precision, preferred_element_type=j...  35.7 us
    psum x1, blocking collectives, local(): squares = lax.psum(jnp.sum(right * right, axis=0), 'tp')  14.2 us

profile of v2, /device:TPU:1, one launch (start us, length us, event | category | flops | bytes accessed | tf_op | source)
XLA Modules:
  0.0 284.1 jit_solution(305989492852896924)
XLA Ops:
  0.6 228.6 %factors.1 = (f32[512,1024]{1,0:T(8,128)}, f32[1792,1024]{1,0:T(8,128)}, f32[1024,1024]{1,0:T(8,128)}) custom-call(f32[512,1792]{1,0:T(8,128)} %momentum_ref.1, bf16[512,1792]{1,0:T(8,128)(2,1)} %gradient_ref.1, f32[112,1024]{1,0:T(8,128)} %basis_ref.1), custom_call_target="tpu_custom_call" | custom-call | flops 60000002048 | bytes 31457280 | tf_op jit(solution)/shard_map/factors/pallas_call | solution.py:465
  229.3 0.0 copy-start.1
  229.3 6.6 %fusion.5 = f32[512,1024]{1,0:T(8,128)S(1)} fusion(f32[512,1024]{1,0:T(8,128)} %get-tuple-element.6, f32[1024,1024]{1,0:T(8,128)} %get-tuple-element.7), kind=kOutput, calls=%fused_computation.10 | convolution fusion | flops 3221225472 | bytes 8388608 | tf_op jit(solution)/shard_map/dot_general | solution.py:25
  235.9 0.0 copy-done.1
  235.9 0.0 copy-start.2
  236.0 0.0 copy-start.3
  236.0 14.7 %multiply_reduce_fusion = (f32[1024]{0:T(1024)S(1)}, f32[1792,1024]{1,0:T(8,128)S(1)}) fusion(f32[1792,1024]{1,0:T(8,128)} %get-tuple-element.8, f32[1024,1024]{1,0:T(8,128)S(1)} %copy-done.1), kind=kOutput, calls=%fused_computation | convolution fusion | flops 11277958144 | bytes 18878464 | tf_op jit(solution)/shard_map/dot_general | solution.py:25
  250.7 0.0 copy-start
  250.7 3.0 %copy-done = f32[1792,1024]{1,0:T(8,128)} copy-done((f32[1792,1024]{1,0:T(8,128)}, f32[1792,1024]{1,0:T(8,128)S(1)}, u32[]{:S(2)}) %copy-start) | copy-done | bytes 7340056
  253.6 0.0 copy-done.2
  253.6 0.0 copy-done.3
  253.6 4.1 %multiply_subtract_fusion = f32[512,1792]{1,0:T(8,128)} fusion(f32[512,1792]{1,0:T(8,128)S(1)} %copy-done.2, bf16[512,1792]{1,0:T(8,128)(2,1)S(1)} %copy-done.3, f32[512,1024]{1,0:T(8,128)S(1)} %fusion.5, f32[1792,1024]{1,0:T(8,128)S(1)} %get-tuple-element.10), kind=kOutput, calls=%fused_computation.1 | convolution fusion | flops 1882718208 | bytes 18612224 | tf_op jit(solution)/shard_map/dot_general | solution.py:25
  257.7 14.2 %psum.7 = f32[1024]{0:T(1024)S(1)} all-reduce(f32[1024]{0:T(1024)S(1)} %get-tuple-element.9), channel_id=1, replica_groups=mesh['fsdp'=16,'tp'=8] {'tp'}, use_global_device_ids=true, to_apply=%region_1.0 | all-reduce | flops 1024 | bytes 8192 | tf_op jit(solution)/shard_map/psum | solution.py:507
  271.9 1.8 dynamic-slice_divide_fusion
  273.8 10.3 %convolution_convert_fusion = bf16[512,1792]{1,0:T(8,128)(2,1)} fusion(f32[1792,1024]{1,0:T(8,128)} %copy-done, f32[512,1024]{1,0:T(8,128)S(1)} %fusion.5, f32[1024]{0:T(1024)S(1)} %add_sqrt_fusion), kind=kOutput, calls=%fused_computation.2 | convolution fusion | flops 5639110656 | bytes 11276288 | tf_op jit(solution)/shard_map/dot_general | solution.py:25
  (1 shorter events, 0.0 us)
Async XLA Ops:
  229.3 6.7 %copy-start.1 = (f32[1024,1024]{1,0:T(8,128)S(1)}, f32[1024,1024]{1,0:T(8,128)}, u32[]{:S(2)}) copy-start(f32[1024,1024]{1,0:T(8,128)} %get-tuple-element.7) | copy-start | bytes 12582916
  235.9 17.7 %copy-start.2 = (f32[512,1792]{1,0:T(8,128)S(1)}, f32[512,1792]{1,0:T(8,128)}, u32[]{:S(2)}) copy-start(f32[512,1792]{1,0:T(8,128)} %momentum_ref.1) | copy-start | bytes 11010052
  236.0 17.7 %copy-start.3 = (bf16[512,1792]{1,0:T(8,128)(2,1)S(1)}, bf16[512,1792]{1,0:T(8,128)(2,1)}, u32[]{:S(2)}) copy-start(bf16[512,1792]{1,0:T(8,128)(2,1)} %gradient_ref.1) | copy-start | bytes 5505028
  250.7 3.0 %copy-start = (f32[1792,1024]{1,0:T(8,128)}, f32[1792,1024]{1,0:T(8,128)S(1)}, u32[]{:S(2)}) copy-start(f32[1792,1024]{1,0:T(8,128)S(1)} %get-tuple-element.10) | copy-start | bytes 22020100

commit v3 on v2

--- a/solution.py
+++ b/solution.py
@@ -297,8 +297,8 @@
 
 
 def main_kernel(
-    momentum_ref, gradient_ref, basis_ref, left_ref, cross_ref, inverse_ref,
-    buf, mh, ml, lbuf, lc, la, lb, lh, ll, ra, rb, rc, rd, held, gpart, gsum, send_sem, recv_sem,
+    momentum_ref, gradient_ref, basis_ref, rh, rl, oh, sh, sl, basis_out,
+    momentum_in, gradient_in, in_sem, left_ref, cross_ref, ih, il, sq, buf, mh, ml, lbuf, lc, la, lb, lh, ll, ra, rb, rc, rd, held, gpart, gsum, send_sem, recv_sem,
 ):
     net = Net(send_sem, recv_sem)
     me = net.y * 4 + net.z
@@ -306,20 +306,33 @@
     barrier = pltpu.get_barrier_semaphore()
     for i in range(1, 16):
         pl.semaphore_signal(barrier, inc=1, device_id=((me + i) % 16, tp), device_id_type=MESH)
-    near = ({"x": 1}, {"x": -1}, {"core": 1})
-    for to in near:
-        pl.semaphore_signal(barrier, inc=1, device_id=net.at(**to), device_id_type=MESH)
-    pl.semaphore_wait(barrier, 15 + len(near))
+    for i in range(1, 8):
+        pl.semaphore_signal(barrier, inc=1, device_id=(me, (tp + i) % 8), device_id_type=MESH)
+    pl.semaphore_wait(barrier, 15 + 7)
 
     events = gather_events(net, "basis", lambda half: basis_ref.at[:, pl.ds(half * WIDE, WIDE)], buf)
     for event in events[:2]:
         event()
     buf[pl.ds(pl.multiple_of(me * SHARD, 8), SHARD), :] = basis_ref[...]
 
-    @pl.loop(0, 16)
-    def _(i):
-        rows = pl.ds(pl.multiple_of(i * 32, 32), 32)
-        mh[rows, :], ml[rows, :] = split(momentum_ref[rows, :] + gradient_ref[rows, :].astype(jnp.float32))
+    def load(i, slot):
+        rows = pl.ds(pl.multiple_of(i * 64, 64), 64)
+        return (
+            pltpu.make_async_copy(momentum_ref.at[rows, :], momentum_in.at[slot], in_sem.at[0, slot]),
+            pltpu.make_async_copy(gradient_ref.at[rows, :], gradient_in.at[slot], in_sem.at[1, slot]),
+        )
+
+    for i in range(8):
+        if i == 0:
+            for copy in load(0, 0):
+                copy.start()
+        if i < 7:
+            for copy in load(i + 1, (i + 1) % 2):
+                copy.start()
+        for copy in load(i, i % 2):
+            copy.wait()
+        rows = slice(64 * i, 64 * i + 64)
+        mh[rows, :], ml[rows, :] = split(momentum_in[i % 2] + gradient_in[i % 2].astype(jnp.float32))
 
     for event in events[2:]:
         event()
@@ -358,8 +371,6 @@
         buf[columns, :] = dot3(mh[:, columns], ml[:, columns], lh[...], ll[...], 0, 0)
 
     scatter = scatter_events(net, "scatter", buf, ra, rb, rc, rd)
-    for event in scatter[:8]:
-        event()
     for copy in copies:
         copy.wait()
     total = gpart[pl.ds(pl.multiple_of(me * 8, 8), 8), :]
@@ -380,7 +391,7 @@
             )
         )
         copies[-1].start()
-    for event in scatter[8:12]:
+    for event in scatter[:12]:
         event()
     for copy in copies:
         copy.wait()
@@ -406,11 +417,53 @@
         cross_ref[rows, :] = buf[rows, :]
 
     rest = scatter[22:] + [keep] + gather_events(net, "cross", own, cross_ref)
-    eliminate(net, held, inverse_ref, rest)
+    eliminate(net, held, ih, il, rest)
     net.sent()
 
-
-def eliminate(net, held, out_ref, events):
+    sq[0] = jnp.zeros((8, RANK), jnp.float32)
+
+    @pl.loop(0, 7)
+    def _(i):
+        rows = pl.ds(pl.multiple_of(i * 256, 256), 256)
+        wh, wl = split(cross_ref[rows, :])
+        for n in range(4):
+            upto = 256 * (n + 1)
+            block = slice(256 * n, upto)
+            part = dot3(wh[:, :upto], wl[:, :upto], ih[block, :upto], il[block, :upto], 1, 1)
+            rh[rows, block], rl[rows, block] = split(part)
+            sq[0, :, block] = sq[0, :, block] + jnp.sum((part * part).reshape(32, 8, 256), axis=0)
+
+    copies = []
+    for i in range(1, 8):
+        copies.append(
+            pltpu.make_async_remote_copy(
+                src_ref=sq.at[0],
+                dst_ref=sq.at[i],
+                send_sem=send_sem.at[190 + i],
+                recv_sem=recv_sem.at[190 + i],
+                device_id=(me, (tp + i) % 8),
+                device_id_type=MESH,
+            )
+        )
+        copies[-1].start()
+    for n in range(4):
+        upto = 256 * (n + 1)
+        block = slice(256 * n, upto)
+        lbuf[:, block] = dot3(lh[:, :upto], ll[:, :upto], ih[block, :upto], il[block, :upto], 1, 1)
+    oh[...] = (0.05 * lbuf[...]).astype(jnp.bfloat16)
+    for copy in copies:
+        copy.wait()
+    total = sq[0]
+    for i in range(1, 8):
+        total = total + sq[i]
+    over = 1.0 / jnp.sqrt(jnp.sum(total, axis=0, keepdims=True) + 1e-08)
+    scale = jnp.sqrt(jnp.float32(M) * jnp.float32(N) / jnp.float32(RANK))
+    sh[...], sl[...] = split(lbuf[...] * (scale * over))
+    rows = pl.ds(pl.multiple_of(me * SHARD, 16), SHARD)
+    basis_out[...] = (rh[rows, :].astype(jnp.float32) + rl[rows, :].astype(jnp.float32)) * over
+
+
+def eliminate(net, held, ih, il, events):
     n = held.shape[0]
     count = n // BLOCK
     shape = (BLOCK, BLOCK)
@@ -443,7 +496,7 @@
         inverse = factor(held[mine, mine], pause)
         held[mine, mine] = eye
         held[mine, :] = dot(inverse, held[mine, :], 1, 0, HIGHEST)
-        out_ref[mine, :] = jnp.where(lanes < (k + 1) * BLOCK, held[mine, :], 0.0)
+        ih[mine, :], il[mine, :] = split(jnp.where(lanes < (k + 1) * BLOCK, held[mine, :], 0.0))
         pause()
 
         def below(t, inner):
@@ -465,13 +518,24 @@
     return pl.pallas_call(
         main_kernel,
         out_shape=[
-            jax.ShapeDtypeStruct((rows, RANK), f32),
-            jax.ShapeDtypeStruct((columns, RANK), f32),
-            jax.ShapeDtypeStruct((RANK, RANK), f32),
+            jax.ShapeDtypeStruct((columns, RANK), bf16),
+            jax.ShapeDtypeStruct((columns, RANK), bf16),
+            jax.ShapeDtypeStruct((rows, RANK), bf16),
+            jax.ShapeDtypeStruct((rows, RANK), bf16),
+            jax.ShapeDtypeStruct((rows, RANK), bf16),
+            jax.ShapeDtypeStruct((SHARD, RANK), f32),
         ],
-        in_specs=[vmem] * 3,
-        out_specs=[vmem] * 3,
+        in_specs=[pl.BlockSpec(memory_space=pl.ANY)] * 2 + [vmem],
+        out_specs=[vmem] * 6,
         scratch_shapes=[
+            pltpu.VMEM((2, 64, columns), f32),
+            pltpu.VMEM((2, 64, columns), bf16),
+            pltpu.SemaphoreType.DMA((2, 2)),
+            pltpu.VMEM((rows, RANK), f32),
+            pltpu.VMEM((columns, RANK), f32),
+            pltpu.VMEM((RANK, RANK), bf16),
+            pltpu.VMEM((RANK, RANK), bf16),
+            pltpu.VMEM((8, 8, RANK), f32),
             pltpu.VMEM((columns, RANK), f32),
             pltpu.VMEM((rows, columns), bf16),
             pltpu.VMEM((rows, columns), bf16),
@@ -488,29 +552,48 @@
             pltpu.VMEM((RANK, RANK), f32),
             pltpu.VMEM((BLOCK, RANK), f32),
             pltpu.VMEM((16, 8, RANK), f32),
-            pltpu.SemaphoreType.DMA((192,)),
-            pltpu.SemaphoreType.DMA((192,)),
+            pltpu.SemaphoreType.DMA((200,)),
+            pltpu.SemaphoreType.DMA((200,)),
         ],
         compiler_params=pltpu.CompilerParams(
-            collective_id=0, has_side_effects=True, vmem_limit_bytes=62 << 20
+            collective_id=0, has_side_effects=True, vmem_limit_bytes=63 << 20
         ),
         cost_estimate=pl.CostEstimate(flops=60_000_000_000, bytes_accessed=30 << 20, transcendentals=0),
         name="factors",
     )(momentum, gradient, basis)
 
 
+def output_kernel(momentum_ref, gradient_ref, rh_ref, rl_ref, oh_ref, sh_ref, sl_ref, momentum_out, update_out):
+    rh, rl = rh_ref[...], rl_ref[...]
+    dims = (((1,), (1,)), ((), ()))
+    low = lax.dot_general(oh_ref[...], rh, dims, preferred_element_type=jnp.float32)
+    momentum_out[...] = (momentum_ref[...] + gradient_ref[...].astype(jnp.float32)) - low
+    update_out[...] = dot3(sh_ref[...], sl_ref[...], rh, rl, 1, 1).astype(jnp.bfloat16)
+
+
+def outputs(momentum, gradient, rh, rl, oh, sh, sl):
+    rows, columns = momentum.shape
+    wide = 256
+    tile = pl.BlockSpec((rows, wide), lambda i: (0, i))
+    right = pl.BlockSpec((wide, RANK), lambda i: (i, 0))
+    whole = pl.BlockSpec((rows, RANK), lambda i: (0, 0))
+    return pl.pallas_call(
+        output_kernel,
+        grid=(columns // wide,),
+        out_shape=[
+            jax.ShapeDtypeStruct((rows, columns), jnp.float32),
+            jax.ShapeDtypeStruct((rows, columns), jnp.bfloat16),
+        ],
+        in_specs=[tile, tile, right, right, whole, whole, whole],
+        out_specs=[tile, tile],
+        compiler_params=pltpu.CompilerParams(vmem_limit_bytes=32 << 20),
+        name="outputs",
+    )(momentum, gradient, rh, rl, oh, sh, sl)
+
+
 def local(gradient, momentum, basis):
-    mixed = momentum + gradient.astype(jnp.float32)
-    left, cross, inverse = factors(momentum, gradient, basis)
-    right = dot(cross, inverse, 1, 1, HIGH)
-    ortho = dot(left, inverse, 1, 1, HIGH)
-    squares = lax.psum(jnp.sum(right * right, axis=0), "tp")
-    new_momentum = mixed - 0.05 * dot(ortho, right, 1, 1, lax.Precision.DEFAULT)
-    colnorm = jnp.sqrt(squares + 1e-08)
-    first = lax.axis_index("fsdp") * SHARD
-    new_basis = lax.dynamic_slice_in_dim(right, first, SHARD, 0) / colnorm
-    scale = jnp.sqrt(jnp.float32(M) * jnp.float32(N) / jnp.float32(RANK))
-    update = dot(scale * ortho / colnorm, right, 1, 1, HIGH).astype(jnp.bfloat16)
+    rh, rl, oh, sh, sl, new_basis = factors(momentum, gradient, basis)
+    new_momentum, update = outputs(momentum, gradient, rh, rl, oh, sh, sl)
     return (new_momentum, new_basis, update)
 
 

time: 284 us -> 261 us (0.919)
  matrix products: 35.7 us -> 0 us
  Pallas kernels: 229 us -> 247 us
  blocking collectives: 14.2 us -> 0 us
  local copies, waits for them, and re-layouts: 2.97 us -> 12.1 us
    dot_general x4 -> x0, matrix products: 35.7 us -> none  [dot(): lax.dot_general(a, b, dims, precision=precision, preferred_element_type=j...]
    pallas_call x1 -> x2, Pallas kernels: 229 us -> 247 us  [the longest x1 237 us: factors(): pl.pallas_call(main_kernel, out_shape=[jax.ShapeDtypeStruct((columns, RAN...]
    psum x1 -> x0, blocking collectives: 14.2 us -> none  [local(): squares = lax.psum(jnp.sum(right * right, axis=0), 'tp')]
    unnamed x8 -> x17, local copies, waits for them, and re-layouts: 2.97 us -> 12.1 us
where the time goes in v3:
time: 261 us; the launch traced here: 260 us
  Pallas kernels  247 us (95%)
  local copies, waits for them, and re-layouts  12.1 us (5%)
    pallas_call x1, Pallas kernels, factors(): pl.pallas_call(main_kernel, out_shape=[jax.ShapeDtypeStruct((columns, RAN...  237 us
    unnamed x17, local copies, waits for them, and re-layouts  12.1 us
    pallas_call x1, Pallas kernels, outputs(): pl.pallas_call(output_kernel, grid=(columns // wide,), out_shape=[jax.Sha...  10.2 us

profile of v3, /device:TPU:1, one launch (start us, length us, event | category | flops | bytes accessed | tf_op | source)
XLA Modules:
  0.0 260.2 jit_solution(5768704497704513007)
XLA Ops:
  0.6 237.3 %factors.1 = (bf16[1792,1024]{1,0:T(8,128)(2,1)}, bf16[1792,1024]{1,0:T(8,128)(2,1)}, bf16[512,1024]{1,0:T(8,128)(2,1)}, bf16[512,1024]{1,0:T(8,128)(2,1)}, bf16...) custom-call(f32[512,1792]{1,0:T(8,128)} %momentum_ref.3, bf16[512,1792]{1,0:T(8,128)(2,1)} %gradient_ref.3, f32[112,1024]{1,0:T(8,128)} %basis_ref.1), custom_call_target="tpu_custom_call" | custom-call | flops 60000002048 | bytes 31457280 | tf_op jit(solution)/shard_map/factors/pallas_call | solution.py:518
  237.9 0.0 copy-start
  237.9 2.0 copy-done
  239.9 0.0 copy-start.1
  239.9 2.0 copy-done.1
  242.0 0.0 copy-start.2
  242.0 2.0 copy-done.2
  244.0 0.0 copy-start.3
  244.0 1.5 copy-done.3
  245.5 0.0 copy-start.4
  245.5 1.2 copy-done.4
  246.7 0.0 copy-start.5
  246.7 1.2 copy-done.5
  248.0 0.0 copy-start.6
  248.0 1.2 copy-done.6
  249.2 0.0 copy-start.7
  249.2 10.2 %outputs.1 = (f32[512,1792]{1,0:T(8,128)}, bf16[512,1792]{1,0:T(8,128)(2,1)}) custom-call(f32[512,1792]{1,0:T(8,128)S(1)} %copy-done, bf16[512,1792]{1,0:T(8,128)(2,1)S(1)} %copy-done.3, bf16[1792,1024]{1,0:T(8,128)(2,1)S(1)} %copy-done.1, bf16[1792,1024]{1,0:T(8,128)(2,1)S(1)} %copy-done.2, bf16[512,1024]{1,0:T(8,128)(2,1)S(1)} %copy-done.4, ...), custom_call_target="tpu_custom_call" | custom-call | tf_op jit(solution)/shard_map/outputs/pallas_call | solution.py:580
  259.4 0.0 copy-done.7
  259.4 0.8 copy.7
Async XLA Ops:
  237.9 2.0 copy-start
  239.9 2.0 copy-start.1
  242.0 2.0 copy-start.2
  244.0 1.5 copy-start.3
  245.5 1.2 copy-start.4
  246.7 1.2 copy-start.5
  248.0 1.2 copy-start.6
  249.2 10.2 %copy-start.7 = (f32[112,1024]{1,0:T(8,128)S(1)}, f32[112,1024]{1,0:T(8,128)}, u32[]{:S(2)}) copy-start(f32[112,1024]{1,0:T(8,128)} %get-tuple-element.23) | copy-start | bytes 1376260

commit v4 on v3

--- a/solution.py
+++ b/solution.py
@@ -128,122 +128,129 @@
         self.open = [key for key in self.open if key not in done]
 
 
-def shard_of(net, ref, first, o1, o2, half, part):
+def shard_of(net, ref, first, o1, o2, columns, part):
     dy, dz = (o1, o2) if first == "y" else (o2, o1)
     index = ((net.y + dy + 4) % 4) * 4 + (net.z + dz + 4) % 4
     at, rows = {"all": (0, SHARD), "top": (0, HALF), "low": (HALF, HALF)}[part]
-    return ref.at[pl.ds(pl.multiple_of(index * SHARD + at, 8), rows), pl.ds(half * WIDE, WIDE)]
-
-
-def gather_events(net, name, own, buf):
-    lists = []
-    for half, (d1, d2) in enumerate((("y", "z"), ("z", "y"))):
-        key = lambda *k, half=half: (name, half) + k
-        shard = lambda o1, o2, part="all", d1=d1, half=half: shard_of(net, buf, d1, o1, o2, half, part)
-
-        def both(o, key=key, shard=shard, d2=d2):
-            for way, sign in ((1, "+"), (-1, "-")):
-                net.send(key(2, o, sign), lambda: shard(o, 0), lambda: shard(o, 0), {d2: way})
-
-        def start(key=key, shard=shard, d1=d1, d2=d2, half=half):
-            mine = lambda: own(half)
-            for way, sign in ((1, "+"), (-1, "-")):
-                net.send(key(1, sign), mine, lambda: shard(0, 0), {d1: way})
-            for way, sign in ((1, "+"), (-1, "-")):
-                net.send(key(2, 0, sign), mine, lambda: shard(0, 0), {d2: way})
-
-        def near(o, way, sign, part, key=key, shard=shard, d1=d1, both=both):
-            net.got(key(1, sign))
-            net.send(key(1, "f" + sign), lambda: shard(o, 0, part), lambda: shard(o, 0, part), {d1: way})
-            both(o)
-
-        def far(key=key, both=both):
-            net.got(key(1, "f+"), key(1, "f-"))
-            both(2)
-
-        def pass_on(o, p, way, sign, part, key=key, shard=shard, d2=d2):
-            net.got(key(2, o, sign))
-            net.send(key(2, o, "f" + sign), lambda: shard(o, p, part), lambda: shard(o, p, part), {d2: way})
-
-        def last(key=key):
-            for o in (0, -1, 1, 2):
-                net.got(key(2, o, "f+"), key(2, o, "f-"))
-
-        events = [start, functools.partial(near, -1, 1, "+", "top"), functools.partial(near, 1, -1, "-", "low")]
-        for i, o in enumerate((0, -1, 1, 2)):
-            if i == 1:
-                events.append(far)
-            events.append(functools.partial(pass_on, o, -1, 1, "+", "top"))
-            events.append(functools.partial(pass_on, o, 1, -1, "-", "low"))
-        events.append(last)
-        lists.append(events)
-    return [e for pair in zip(*lists) for e in pair]
-
-
-def scatter_events(net, name, buf, ra, rb, rc, rd):
-    lists = []
+    return ref.at[pl.ds(pl.multiple_of(index * SHARD + at, 8), rows), columns]
+
+
+def both_lists(one, other):
+    order = [((i + 0.5) / len(one), 0, i) for i in range(len(one))]
+    order += [((i + 0.5) / len(other), 1, i) for i in range(len(other))]
+    return [(one, other)[which][i] for _, which, i in sorted(order)]
+
+
+def gather_events(net, name, own, buf, d1, d2, columns):
+    def key(*k):
+        return (name, d1) + k
+
+    def shard(o1, o2, part="all"):
+        return shard_of(net, buf, d1, o1, o2, columns, part)
+
+    def both(o):
+        for way, sign in ((1, "+"), (-1, "-")):
+            net.send(key(2, o, sign), lambda: shard(o, 0), lambda: shard(o, 0), {d2: way})
+
+    def start():
+        for way, sign in ((1, "+"), (-1, "-")):
+            net.send(key(1, sign), own, lambda: shard(0, 0), {d1: way})
+        for way, sign in ((1, "+"), (-1, "-")):
+            net.send(key(2, 0, sign), own, lambda: shard(0, 0), {d2: way})
+
+    def near(o, way, sign, part):
+        net.got(key(1, sign))
+        net.send(key(1, "f" + sign), lambda: shard(o, 0, part), lambda: shard(o, 0, part), {d1: way})
+        both(o)
+
+    def far():
+        net.got(key(1, "f+"), key(1, "f-"))
+        both(2)
+
+    def pass_on(o, p, way, sign, part):
+        net.got(key(2, o, sign))
+        net.send(key(2, o, "f" + sign), lambda: shard(o, p, part), lambda: shard(o, p, part), {d2: way})
+
+    def last():
+        for o in (0, -1, 1, 2):
+            net.got(key(2, o, "f+"), key(2, o, "f-"))
+
+    events = [start, functools.partial(near, -1, 1, "+", "top"), functools.partial(near, 1, -1, "-", "low")]
+    for i, o in enumerate((0, -1, 1, 2)):
+        if i == 1:
+            events.append(far)
+        events.append(functools.partial(pass_on, o, -1, 1, "+", "top"))
+        events.append(functools.partial(pass_on, o, 1, -1, "-", "low"))
+    events.append(last)
+    return events
+
+
+def scatter_events(net, name, buf, ra, rb, rc, rd, e1, e2, half):
     order = (2, 1, -1, 0)
-    for half, (e1, e2) in enumerate((("y", "z"), ("z", "y"))):
-        key = lambda *k, half=half: (name, half) + k
-        shard = lambda o1, o2, part="all", e1=e1, half=half: shard_of(net, buf, e1, o1, o2, half, part)
-
-        def add(ref, *others):
-            if net.dry:
-                return
-            total = ref[...]
-            for other in others:
-                total = total + other[...]
-            ref[...] = total
-
-        def start(o, key=key, shard=shard, e1=e1, half=half):
-            i = (half * 4 + order.index(o)) * 2
-            net.send(key(1, o, "f+"), lambda: shard(2, o, "top"), lambda: ra.at[i], {e1: 1})
-            net.send(key(1, o, "f-"), lambda: shard(2, o, "low"), lambda: ra.at[i + 1], {e1: -1})
-
-        def near(o, way, sign, part, j, key=key, shard=shard, e1=e1, half=half):
-            i = (half * 4 + order.index(o)) * 2 + j
-            net.got(key(1, o, "f" + sign))
-            add(shard(way, o, part), ra.at[i])
-            net.send(key(1, o, sign), lambda: shard(way, o), lambda: rb.at[i], {e1: way})
-
-        def line(o, key=key, shard=shard, half=half):
-            i = (half * 4 + order.index(o)) * 2
-            net.got(key(1, o, "+"), key(1, o, "-"))
-            add(shard(0, o), rb.at[i], rb.at[i + 1])
-
-        def far(key=key, shard=shard, e2=e2, half=half, line=line):
-            line(2)
-            net.send(key(2, "f+"), lambda: shard(0, 2, "top"), lambda: rc.at[2 * half], {e2: 1})
-            net.send(key(2, "f-"), lambda: shard(0, 2, "low"), lambda: rc.at[2 * half + 1], {e2: -1})
-
-        def side(way, sign, part, j, key=key, shard=shard, e2=e2, half=half, line=line):
-            line(way)
-            net.got(key(2, "f" + sign))
-            add(shard(0, way, part), rc.at[2 * half + j])
-            net.send(key(2, sign), lambda: shard(0, way), lambda: rd.at[2 * half + j], {e2: way})
-
-        def mine(key=key, shard=shard, half=half, line=line):
-            line(0)
-            net.got(key(2, "+"), key(2, "-"))
-            add(shard(0, 0), rd.at[2 * half], rd.at[2 * half + 1])
-
-        events = [functools.partial(start, o) for o in order]
-        for o in order:
-            events.append(functools.partial(near, o, 1, "+", "top", 0))
-            events.append(functools.partial(near, o, -1, "-", "low", 1))
-            if o == 1:
-                events.append(far)
-        events.append(functools.partial(side, 1, "+", "top", 0))
-        events.append(functools.partial(side, -1, "-", "low", 1))
-        events.append(mine)
-        lists.append(events)
-    return [e for pair in zip(*lists) for e in pair]
-
-
-def tp_gather_events(net, name, ref, piece, start_of):
+    columns = pl.ds(half * WIDE, WIDE)
+
+    def key(*k):
+        return (name, e1) + k
+
+    def shard(o1, o2, part="all"):
+        return shard_of(net, buf, e1, o1, o2, columns, part)
+
+    def slot(o):
+        return (half * 4 + order.index(o)) * 2
+
+    def add(ref, *others):
+        if net.dry:
+            return
+        total = ref[...]
+        for other in others:
+            total = total + other[...]
+        ref[...] = total
+
+    def start(o):
+        net.send(key(1, o, "f+"), lambda: shard(2, o, "top"), lambda: ra.at[slot(o)], {e1: 1})
+        net.send(key(1, o, "f-"), lambda: shard(2, o, "low"), lambda: ra.at[slot(o) + 1], {e1: -1})
+
+    def near(o, way, sign, part, j):
+        net.got(key(1, o, "f" + sign))
+        add(shard(way, o, part), ra.at[slot(o) + j])
+        net.send(key(1, o, sign), lambda: shard(way, o), lambda: rb.at[slot(o) + j], {e1: way})
+
+    def line(o):
+        net.got(key(1, o, "+"), key(1, o, "-"))
+        add(shard(0, o), rb.at[slot(o)], rb.at[slot(o) + 1])
+
+    def far():
+        line(2)
+        net.send(key(2, "f+"), lambda: shard(0, 2, "top"), lambda: rc.at[2 * half], {e2: 1})
+        net.send(key(2, "f-"), lambda: shard(0, 2, "low"), lambda: rc.at[2 * half + 1], {e2: -1})
+
+    def side(way, sign, part, j):
+        line(way)
+        net.got(key(2, "f" + sign))
+        add(shard(0, way, part), rc.at[2 * half + j])
+        net.send(key(2, sign), lambda: shard(0, way), lambda: rd.at[2 * half + j], {e2: way})
+
+    def mine():
+        line(0)
+        net.got(key(2, "+"), key(2, "-"))
+        add(shard(0, 0), rd.at[2 * half], rd.at[2 * half + 1])
+
+    events = [functools.partial(start, o) for o in order]
+    for o in order:
+        events.append(functools.partial(near, o, 1, "+", "top", 0))
+        events.append(functools.partial(near, o, -1, "-", "low", 1))
+        if o == 1:
+            events.append(far)
+    events.append(functools.partial(side, 1, "+", "top", 0))
+    events.append(functools.partial(side, -1, "-", "low", 1))
+    events.append(mine)
+    return events
+
+
+def tp_gather_events(net, name, ref, piece, start_of, columns=slice(None)):
     def part(dx, which="all"):
         at, rows = {"all": (0, piece), "top": (0, piece // 2), "low": (piece // 2, piece // 2)}[which]
-        return ref.at[pl.ds(pl.multiple_of(start_of(dx) + at, 8), rows), :]
+        return ref.at[pl.ds(pl.multiple_of(start_of(dx) + at, 8), rows), columns]
 
     def put(key, dx, which, to):
         net.send((name,) + key, lambda: part(dx, which), lambda: part(dx, which), to)
@@ -269,31 +276,48 @@
     return start, near, last
 
 
-def tp_sum(net, ref, out, lc, la, lb):
+def tp_sum_events(net, ref, out, lc, la, lb, half):
     mine = net.core * 256
-    other = 256 - mine
-    net.send(("core",), lambda: ref.at[pl.ds(pl.multiple_of(other, 8), 256), :], lambda: lc, {"core": 1})
-    net.got(("core",))
-    rows = pl.ds(pl.multiple_of(mine, 8), 256)
-    ref[rows, :] = ref[rows, :] + lc[...]
+    columns = pl.ds(half * WIDE, WIDE)
+
+    def key(k):
+        return ("sum", half, k)
+
+    def rows_at(at, count, of=ref):
+        return of.at[pl.ds(pl.multiple_of(at, 8), count), columns]
 
     def start_of(dx):
         return mine + ((net.x + dx + 4) % 4) * 64
 
     def piece(dx, at=0, count=64):
-        return ref.at[pl.ds(pl.multiple_of(start_of(dx) + at, 8), count), :]
-
-    net.send(("xf+",), lambda: piece(2, 0, 32), lambda: la.at[0], {"x": 1})
-    net.send(("xf-",), lambda: piece(2, 32, 32), lambda: la.at[1], {"x": -1})
-    for way, sign, at, j in ((1, "+", 0, 0), (-1, "-", 32, 1)):
-        net.got(("xf" + sign,))
-        there = piece(way, at, 32)
-        there[...] = there[...] + la[j]
-        net.send(("x" + sign,), lambda way=way: piece(way), lambda j=j: lb.at[j], {"x": way})
-    net.got(("x+",), ("x-",))
-    out[pl.ds(pl.multiple_of(start_of(0), 8), 64), :] = piece(0)[...] + lb[0] + lb[1]
-    for event in tp_gather_events(net, "left", out, 64, start_of):
-        event()
+        return rows_at(start_of(dx) + at, count)
+
+    def start():
+        net.send(key("core"), lambda: rows_at(256 - mine, 256), lambda: lc.at[half], {"core": 1})
+
+    def pair():
+        net.got(key("core"))
+        there = rows_at(mine, 256)
+        there[...] = there[...] + lc[half]
+        net.send(key("f+"), lambda: piece(2, 0, 32), lambda: la.at[half, 0], {"x": 1})
+        net.send(key("f-"), lambda: piece(2, 32, 32), lambda: la.at[half, 1], {"x": -1})
+
+    def side():
+        for way, sign, at, j in ((1, "+", 0, 0), (-1, "-", 32, 1)):
+            net.got(key("f" + sign))
+            there = piece(way, at, 32)
+            there[...] = there[...] + la[half, j]
+            net.send(key(sign), lambda way=way: piece(way), lambda j=j: lb.at[half, j], {"x": way})
+
+    gather = tp_gather_events(net, "left%d" % half, out, 64, start_of, columns)
+
+    def own():
+        net.got(key("+"), key("-"))
+        there = rows_at(start_of(0), 64, out)
+        there[...] = piece(0)[...] + lb[half, 0] + lb[half, 1]
+        gather[0]()
+
+    return [start, pair, side, own, gather[1], gather[2]]
 
 
 def main_kernel(
@@ -310,9 +334,19 @@
         pl.semaphore_signal(barrier, inc=1, device_id=(me, (tp + i) % 8), device_id_type=MESH)
     pl.semaphore_wait(barrier, 15 + 7)
 
-    events = gather_events(net, "basis", lambda half: basis_ref.at[:, pl.ds(half * WIDE, WIDE)], buf)
-    for event in events[:2]:
-        event()
+    def run(events):
+        for event in events:
+            event()
+
+    gathers = []
+    for half in range(2):
+        lists = []
+        for i, axes in enumerate((("y", "z"), ("z", "y"))):
+            columns = pl.ds(half * WIDE + i * 256, 256)
+            lists.append(gather_events(net, "basis%d" % half, lambda c=columns: basis_ref.at[:, c], buf, *axes, columns))
+        gathers.append(both_lists(*lists))
+    g0, g1 = gathers
+    run(g0[:2])
     buf[pl.ds(pl.multiple_of(me * SHARD, 8), SHARD), :] = basis_ref[...]
 
     def load(i, slot):
@@ -334,17 +368,36 @@
         rows = slice(64 * i, 64 * i + 64)
         mh[rows, :], ml[rows, :] = split(momentum_in[i % 2] + gradient_in[i % 2].astype(jnp.float32))
 
-    for event in events[2:]:
-        event()
-
-    @pl.loop(0, 4)
-    def _(i):
-        columns = pl.ds(pl.multiple_of(i * 256, 256), 256)
-        bh, bl = split(buf[:, columns])
-        lbuf[:, columns] = dot3(mh[...], ml[...], bh, bl, 1, 0)
-
-    tp_sum(net, lbuf, left_ref, lc, la, lb)
-    net.sent()
+    def left_part(half):
+        @pl.loop(0, 2)
+        def _(i):
+            columns = pl.ds(pl.multiple_of(half * WIDE + i * 256, 256), 256)
+            bh, bl = split(buf[:, columns])
+            lbuf[:, columns] = dot3(mh[...], ml[...], bh, bl, 1, 0)
+
+    def cross_part(half):
+        half_columns = slice(half * WIDE, (half + 1) * WIDE)
+        lh[:, half_columns], ll[:, half_columns] = split(left_ref[:, half_columns])
+        net.sent("basis%d" % half)
+
+        @pl.loop(0, 7)
+        def _(i):
+            columns = pl.ds(pl.multiple_of(i * 256, 256), 256)
+            buf[columns, half_columns] = dot3(
+                mh[:, columns], ml[:, columns], lh[:, half_columns], ll[:, half_columns], 0, 0
+            )
+
+    t0, t1 = [tp_sum_events(net, lbuf, left_ref, lc, la, lb, half) for half in range(2)]
+    s0 = scatter_events(net, "scatter", buf, ra, rb, rc, rd, "y", "z", 0)
+    s1 = scatter_events(net, "scatter", buf, ra, rb, rc, rd, "z", "y", 1)
+    run(g0[2:8] + g1[:2] + g0[8:14] + g1[2:6] + g0[14:20] + g1[6:10] + g0[20:])
+    left_part(0)
+    run(t0[:1] + g1[10:14] + t0[1:2] + g1[14:16] + t0[2:3] + g1[16:19])
+    run(t0[3:4] + g1[19:22] + t0[4:5] + g1[22:24] + t0[5:] + g1[24:])
+    left_part(1)
+    run(t1[:1])
+    cross_part(0)
+    run(t1[1:2] + s0[:4] + t1[2:3] + s0[4:6] + t1[3:5] + s0[6:8] + t1[5:])
 
     own_rows = pl.ds(pl.multiple_of(tp * BLOCK, BLOCK), BLOCK)
     gpart[...] = dot(left_ref[:, own_rows], left_ref[...], 0, 0, HIGHEST)
@@ -355,22 +408,15 @@
             pltpu.make_async_remote_copy(
                 src_ref=gpart.at[pl.ds(pl.multiple_of(to * 8, 8), 8), :],
                 dst_ref=gsum.at[i],
-                send_sem=send_sem.at[150 + i],
-                recv_sem=recv_sem.at[150 + i],
+                send_sem=send_sem.at[220 + i],
+                recv_sem=recv_sem.at[220 + i],
                 device_id=(to, tp),
                 device_id_type=MESH,
             )
         )
         copies[-1].start()
 
-    lh[...], ll[...] = split(left_ref[...])
-
-    @pl.loop(0, 7)
-    def _(i):
-        columns = pl.ds(pl.multiple_of(i * 256, 256), 256)
-        buf[columns, :] = dot3(mh[:, columns], ml[:, columns], lh[...], ll[...], 0, 0)
-
-    scatter = scatter_events(net, "scatter", buf, ra, rb, rc, rd)
+    cross_part(1)
     for copy in copies:
         copy.wait()
     total = gpart[pl.ds(pl.multiple_of(me * 8, 8), 8), :]
@@ -384,39 +430,38 @@
             pltpu.make_async_remote_copy(
                 src_ref=held.at[pl.ds(at, 8), :],
                 dst_ref=held.at[pl.ds(at, 8), :],
-                send_sem=send_sem.at[170 + i],
-                recv_sem=recv_sem.at[170 + i],
+                send_sem=send_sem.at[236 + i],
+                recv_sem=recv_sem.at[236 + i],
                 device_id=((me + i) % 16, tp),
                 device_id_type=MESH,
             )
         )
         copies[-1].start()
-    for event in scatter[:12]:
-        event()
+    run(s1[:4] + s0[8:11])
     for copy in copies:
         copy.wait()
     gram_events = tp_gather_events(
         net, "gram", held, BLOCK, lambda dx: (((net.x + dx + 4) % 4) * 2 + net.core) * BLOCK
     )
     gram_events[0]()
-    for event in scatter[12:18]:
-        event()
+    run(s0[11:13] + s1[4:8])
     gram_events[1]()
-    for event in scatter[18:22]:
-        event()
+    run(s0[13:15] + s1[8:11])
     gram_events[2]()
     net.sent("gram")
 
-    def own(half):
-        return shard_of(net, buf, "y", 0, 0, half, "all")
-
-    def keep():
-        if net.dry:
-            return
-        rows = pl.ds(pl.multiple_of(me * SHARD, 8), SHARD)
-        cross_ref[rows, :] = buf[rows, :]
-
-    rest = scatter[22:] + [keep] + gather_events(net, "cross", own, cross_ref)
+    rows = pl.ds(pl.multiple_of(me * SHARD, 8), SHARD)
+
+    def keep(columns):
+        if not net.dry:
+            cross_ref[rows, columns] = buf[rows, columns]
+
+    rest = []
+    for half, axes, begun in ((0, ("y", "z"), s0[15:]), (1, ("z", "y"), s1[11:])):
+        columns = pl.ds(half * WIDE, WIDE)
+        rest.append(begun + [functools.partial(keep, columns)])
+        rest[-1] += gather_events(net, "cross", lambda c=columns: buf.at[rows, c], cross_ref, *axes, columns)
+    rest = both_lists(*rest)
     eliminate(net, held, ih, il, rest)
     net.sent()
 
@@ -439,8 +484,8 @@
             pltpu.make_async_remote_copy(
                 src_ref=sq.at[0],
                 dst_ref=sq.at[i],
-                send_sem=send_sem.at[190 + i],
-                recv_sem=recv_sem.at[190 + i],
+                send_sem=send_sem.at[252 + i],
+                recv_sem=recv_sem.at[252 + i],
                 device_id=(me, (tp + i) % 8),
                 device_id_type=MESH,
             )
@@ -540,9 +585,9 @@
             pltpu.VMEM((rows, columns), bf16),
             pltpu.VMEM((rows, columns), bf16),
             pltpu.VMEM((rows, RANK), f32),
-            pltpu.VMEM((256, RANK), f32),
-            pltpu.VMEM((2, 32, RANK), f32),
-            pltpu.VMEM((2, 64, RANK), f32),
+            pltpu.VMEM((2, 256, WIDE), f32),
+            pltpu.VMEM((2, 2, 32, WIDE), f32),
+            pltpu.VMEM((2, 2, 64, WIDE), f32),
             pltpu.VMEM((rows, RANK), bf16),
             pltpu.VMEM((rows, RANK), bf16),
             pltpu.VMEM((16, HALF, WIDE), f32),
@@ -552,8 +597,8 @@
             pltpu.VMEM((RANK, RANK), f32),
             pltpu.VMEM((BLOCK, RANK), f32),
             pltpu.VMEM((16, 8, RANK), f32),
-            pltpu.SemaphoreType.DMA((200,)),
-            pltpu.SemaphoreType.DMA((200,)),
+            pltpu.SemaphoreType.DMA((260,)),
+            pltpu.SemaphoreType.DMA((260,)),
         ],
         compiler_params=pltpu.CompilerParams(
             collective_id=0, has_side_effects=True, vmem_limit_bytes=63 << 20
@@ -586,7 +631,7 @@
         ],
         in_specs=[tile, tile, right, right, whole, whole, whole],
         out_specs=[tile, tile],
-        compiler_params=pltpu.CompilerParams(vmem_limit_bytes=32 << 20),
+        compiler_params=pltpu.CompilerParams(vmem_limit_bytes=63 << 20),
         name="outputs",
     )(momentum, gradient, rh, rl, oh, sh, sl)
 

time: 261 us -> 261 us (level)
  Pallas kernels: 247 us -> 259 us
  local copies, waits for them, and re-layouts: 12.1 us -> 0.77 us
    unnamed x17 -> x3, local copies, waits for them, and re-layouts: 12.1 us -> 0.77 us
    pallas_call x1, Pallas kernels: 237 us -> 246 us  [factors(): pl.pallas_call(main_kernel, out_shape=[jax.ShapeDtypeStruct((columns, RAN...]
    pallas_call x1, Pallas kernels: 10.2 us -> 13.1 us  [outputs(): pl.pallas_call(output_kernel, grid=(columns // wide,), out_shape=[jax.Sha...]
where the time goes in v4:
time: 261 us; the launch traced here: 260 us
  Pallas kernels  259 us (99%)
    pallas_call x1, Pallas kernels, factors(): pl.pallas_call(main_kernel, out_shape=[jax.ShapeDtypeStruct((columns, RAN...  246 us
    pallas_call x1, Pallas kernels, outputs(): pl.pallas_call(output_kernel, grid=(columns // wide,), out_shape=[jax.Sha...  13.1 us

profile of v4, /device:TPU:1, one launch (start us, length us, event | category | flops | bytes accessed | tf_op | source)
XLA Modules:
  0.0 260.1 jit_solution(5321248862572638051)
XLA Ops:
  0.6 245.5 %factors.1 = (bf16[1792,1024]{1,0:T(8,128)(2,1)}, bf16[1792,1024]{1,0:T(8,128)(2,1)}, bf16[512,1024]{1,0:T(8,128)(2,1)}, bf16[512,1024]{1,0:T(8,128)(2,1)}, bf16...) custom-call(f32[512,1792]{1,0:T(8,128)} %momentum_ref.3, bf16[512,1792]{1,0:T(8,128)(2,1)} %gradient_ref.3, f32[112,1024]{1,0:T(8,128)} %basis_ref.1), custom_call_target="tpu_custom_call" | custom-call | flops 60000002048 | bytes 31457280 | tf_op jit(solution)/shard_map/factors/pallas_call | solution.py:563
  246.2 0.0 copy-start
  246.2 13.1 %outputs.1 = (f32[512,1792]{1,0:T(8,128)}, bf16[512,1792]{1,0:T(8,128)(2,1)}) custom-call(f32[512,1792]{1,0:T(8,128)} %momentum_ref.3, bf16[512,1792]{1,0:T(8,128)(2,1)} %gradient_ref.3, bf16[1792,1024]{1,0:T(8,128)(2,1)} %get-tuple-element.11.rh_ref, bf16[1792,1024]{1,0:T(8,128)(2,1)} %get-tuple-element.12.rl_ref, ...), custom_call_target="tpu_custom_call" | custom-call | tf_op jit(solution)/shard_map/outputs/pallas_call | solution.py:625
  259.3 0.0 copy-done
  259.3 0.8 copy.7
Async XLA Ops:
  246.2 13.2 %copy-start = (f32[112,1024]{1,0:T(8,128)S(1)}, f32[112,1024]{1,0:T(8,128)}, u32[]{:S(2)}) copy-start(f32[112,1024]{1,0:T(8,128)} %get-tuple-element.23) | copy-start | bytes 1376260

commit v5 on v3

--- a/solution.py
+++ b/solution.py
@@ -26,9 +26,8 @@
 
 
 def recip(d):
-    r = pl.reciprocal(d, approx=True)
-    r = r * (2.0 - d * r)
-    return r * (2.0 - d * r)
+    r = lax.rsqrt(d)
+    return r * r
 
 
 def factor(block, pause):
@@ -586,7 +585,7 @@
         ],
         in_specs=[tile, tile, right, right, whole, whole, whole],
         out_specs=[tile, tile],
-        compiler_params=pltpu.CompilerParams(vmem_limit_bytes=32 << 20),
+        compiler_params=pltpu.CompilerParams(vmem_limit_bytes=63 << 20),
         name="outputs",
     )(momentum, gradient, rh, rl, oh, sh, sl)
 

time: 261 us -> 250 us (0.958)
  local copies, waits for them, and re-layouts: 12.1 us -> 0.77 us
    unnamed x17 -> x3, local copies, waits for them, and re-layouts: 12.1 us -> 0.77 us
    pallas_call x1, Pallas kernels: 10.2 us -> 13.1 us  [outputs(): pl.pallas_call(output_kernel, grid=(columns // wide,), out_shape=[jax.Sha...]
    pallas_call x1, Pallas kernels: 237 us -> 235 us  [factors(): pl.pallas_call(main_kernel, out_shape=[jax.ShapeDtypeStruct((columns, RAN...]
where the time goes in v5:
time: 250 us; the launch traced here: 249 us
  Pallas kernels  248 us (99%)
    pallas_call x1, Pallas kernels, factors(): pl.pallas_call(main_kernel, out_shape=[jax.ShapeDtypeStruct((columns, RAN...  235 us
    pallas_call x1, Pallas kernels, outputs(): pl.pallas_call(output_kernel, grid=(columns // wide,), out_shape=[jax.Sha...  13.1 us

profile of v5, /device:TPU:1, one launch (start us, length us, event | category | flops | bytes accessed | tf_op | source)
XLA Modules:
  0.0 249.2 jit_solution(18277000466923977731)
XLA Ops:
  0.6 234.6 %factors.1 = (bf16[1792,1024]{1,0:T(8,128)(2,1)}, bf16[1792,1024]{1,0:T(8,128)(2,1)}, bf16[512,1024]{1,0:T(8,128)(2,1)}, bf16[512,1024]{1,0:T(8,128)(2,1)}, bf16...) custom-call(f32[512,1792]{1,0:T(8,128)} %momentum_ref.3, bf16[512,1792]{1,0:T(8,128)(2,1)} %gradient_ref.3, f32[112,1024]{1,0:T(8,128)} %basis_ref.1), custom_call_target="tpu_custom_call" | custom-call | flops 60000002048 | bytes 31457280 | tf_op jit(solution)/shard_map/factors/pallas_call | solution.py:517
  235.2 0.0 copy-start
  235.3 13.1 %outputs.1 = (f32[512,1792]{1,0:T(8,128)}, bf16[512,1792]{1,0:T(8,128)(2,1)}) custom-call(f32[512,1792]{1,0:T(8,128)} %momentum_ref.3, bf16[512,1792]{1,0:T(8,128)(2,1)} %gradient_ref.3, bf16[1792,1024]{1,0:T(8,128)(2,1)} %get-tuple-element.11.rh_ref, bf16[1792,1024]{1,0:T(8,128)(2,1)} %get-tuple-element.12.rl_ref, ...), custom_call_target="tpu_custom_call" | custom-call | tf_op jit(solution)/shard_map/outputs/pallas_call | solution.py:579
  248.4 0.0 copy-done
  248.4 0.8 copy.7
Async XLA Ops:
  235.2 13.2 %copy-start = (f32[112,1024]{1,0:T(8,128)S(1)}, f32[112,1024]{1,0:T(8,128)}, u32[]{:S(2)}) copy-start(f32[112,1024]{1,0:T(8,128)} %get-tuple-element.23) | copy-start | bytes 1376260

commit v6 on v5

--- a/solution.py
+++ b/solution.py
@@ -390,7 +390,7 @@
             )
         )
         copies[-1].start()
-    for event in scatter[:12]:
+    for event in scatter[:8]:
         event()
     for copy in copies:
         copy.wait()
@@ -398,10 +398,10 @@
         net, "gram", held, BLOCK, lambda dx: (((net.x + dx + 4) % 4) * 2 + net.core) * BLOCK
     )
     gram_events[0]()
-    for event in scatter[12:18]:
+    for event in scatter[8:14]:
         event()
     gram_events[1]()
-    for event in scatter[18:22]:
+    for event in scatter[14:20]:
         event()
     gram_events[2]()
     net.sent("gram")
@@ -415,7 +415,7 @@
         rows = pl.ds(pl.multiple_of(me * SHARD, 8), SHARD)
         cross_ref[rows, :] = buf[rows, :]
 
-    rest = scatter[22:] + [keep] + gather_events(net, "cross", own, cross_ref)
+    rest = scatter[20:] + [keep] + gather_events(net, "cross", own, cross_ref)
     eliminate(net, held, ih, il, rest)
     net.sent()
 

time: 250 us -> 248 us (level)
  no operation moved by 1% of the time
where the time goes in v6:
time: 248 us
  Pallas kernels  246 us (99%)
    pallas_call x1, Pallas kernels, factors(): pl.pallas_call(main_kernel, out_shape=[jax.ShapeDtypeStruct((columns, RAN...  233 us
    pallas_call x1, Pallas kernels, outputs(): pl.pallas_call(output_kernel, grid=(columns // wide,), out_shape=[jax.Sha...  13.1 us

profile of v6, /device:TPU:1, one launch (start us, length us, event | category | flops | bytes accessed | tf_op | source)
XLA Modules:
  0.0 247.8 jit_solution(9656146067697559712)
XLA Ops:
  0.6 233.2 %factors.1 = (bf16[1792,1024]{1,0:T(8,128)(2,1)}, bf16[1792,1024]{1,0:T(8,128)(2,1)}, bf16[512,1024]{1,0:T(8,128)(2,1)}, bf16[512,1024]{1,0:T(8,128)(2,1)}, bf16...) custom-call(f32[512,1792]{1,0:T(8,128)} %momentum_ref.3, bf16[512,1792]{1,0:T(8,128)(2,1)} %gradient_ref.3, f32[112,1024]{1,0:T(8,128)} %basis_ref.1), custom_call_target="tpu_custom_call" | custom-call | flops 60000002048 | bytes 31457280 | tf_op jit(solution)/shard_map/factors/pallas_call | solution.py:517
  233.8 0.0 copy-start
  233.8 13.1 %outputs.1 = (f32[512,1792]{1,0:T(8,128)}, bf16[512,1792]{1,0:T(8,128)(2,1)}) custom-call(f32[512,1792]{1,0:T(8,128)} %momentum_ref.3, bf16[512,1792]{1,0:T(8,128)(2,1)} %gradient_ref.3, bf16[1792,1024]{1,0:T(8,128)(2,1)} %get-tuple-element.11.rh_ref, bf16[1792,1024]{1,0:T(8,128)(2,1)} %get-tuple-element.12.rl_ref, ...), custom_call_target="tpu_custom_call" | custom-call | tf_op jit(solution)/shard_map/outputs/pallas_call | solution.py:579
  247.0 0.0 copy-done
  247.0 0.8 copy.7
Async XLA Ops:
  233.8 13.2 %copy-start = (f32[112,1024]{1,0:T(8,128)S(1)}, f32[112,1024]{1,0:T(8,128)}, u32[]{:S(2)}) copy-start(f32[112,1024]{1,0:T(8,128)} %get-tuple-element.23) | copy-start | bytes 1376260
